TPU v7x, 1024 devices: a whole 4x8x16 slice. The times are simulated.
1024 devices in a mesh: span: 16 (over y, core), head: 16 (over z), rep: 4 (over x).
Axes of the slice: x: 4, y: 8, z: 16, core: 2. Of those that a mesh axis runs over, the one named last changes fastest.
Arguments:
- queries: bfloat16 [131072, 4096], P(('rep', 'span', 'head')), parts along dimension 0, may hold values from -9 to 9
- keys: bfloat16 [131072, 512], P(('rep', 'span', 'head')), parts along dimension 0, may hold values from -9 to 9
- values: bfloat16 [131072, 512], P(('rep', 'span', 'head')), parts along dimension 0, may hold values from -6 to 6
- out_grad: bfloat16 [131072, 4096], P(('rep', 'span'), 'head'), parts along dimension 0, may hold values from -6 to 6
- doc_lengths: int32 [128], P('rep'), parts along dimension 0, may hold values from 1 to 4096, 32768 in all
Outputs:
- key_value_grads: bfloat16 [1024, 131072], P('head', ('rep', 'span')), parts along dimension 1
- log_totals: float32 [32, 131072], P('head', ('rep', 'span')), parts along dimension 1
There are 4 independent parts, one for each index of `rep`. A program takes and returns all parts, laid end to end along the dimension named above; each array names one. Nothing has to cross between parts.
Inputs may be any that keep to these rules, and one draw needn't show every extreme that they name: `doc_lengths`: they sum to 32768; the longest is exactly 4096.
All inputs are finite; a program needn't handle non-finite values.
Results may differ from a plain program's by a relative error of at most 0.0068.
Values may be sent and summed in bfloat16 or wider, within the bound.
No kernel may reach another device: no remote copies, remote signals or barrier semaphores. Data moves between devices by JAX's collectives and lax.ppermute only.
A program may use at most 32 MiB of HBM per device.

v0:
```python
import math

import jax
import jax.numpy as jnp
from jax import lax
from jax.sharding import PartitionSpec as P

HEADS = 32
KV_HEADS = 4
HEAD_DIM = 128
BLOCK = 128
WINDOW = 2
HALO = 128


def from_partner(block, axis, bit):
    count = lax.axis_size(axis)
    route = []
    for low in range(count):
        high = low | 1 << bit
        if high != low and high < count:
            route += [(low, high), (high, low)]
    return lax.ppermute(block, axis, route)


def sent_together(arrays, axis, split_dim, concat_dim, along):
    ends, at = ([], 0)
    for a in arrays[:-1]:
        at += a.shape[along]
        ends.append(at)
    both = jnp.concatenate(arrays, axis=along)
    return tuple(
        jnp.split(
            lax.all_to_all(both, axis, split_axis=split_dim, concat_axis=concat_dim, tiled=True),
            ends,
            axis=along,
        )
    )


def passed_along(block, axis, distance):
    devices = range(lax.axis_size(axis))
    route = [(i - distance, i) for i in devices if i - distance in devices]
    return lax.ppermute(block, axis, route)


def group_total(partial_value, sharers, head_index):
    levels = sharers.bit_length() - 1
    for level in reversed(range(levels)):
        half_rows = partial_value.shape[0] // 2
        lower_half = head_index >> level & 1 == 0
        kept_rows = jnp.where(lower_half, partial_value[:half_rows], partial_value[half_rows:])
        given_rows = jnp.where(lower_half, partial_value[half_rows:], partial_value[:half_rows])
        partial_value = kept_rows + from_partner(
            given_rows.astype(jnp.bfloat16), "head", level
        ).astype(given_rows.dtype)
    return partial_value


def shards(queries, keys, values, out_grad, doc_lengths):
    head_count = lax.axis_size("head")
    head_index = lax.axis_index("head")
    span_index = lax.axis_index("span")
    tok_rows = queries.shape[0]
    heads_here = HEADS // head_count
    sharers = head_count // KV_HEADS
    span_len = tok_rows * head_count
    score_scale = 1.0 / math.sqrt(HEAD_DIM)
    query_send = queries.reshape(tok_rows, head_count, heads_here * HEAD_DIM)
    keyval = jnp.concatenate(
        [keys.reshape(tok_rows, KV_HEADS, HEAD_DIM), values.reshape(tok_rows, KV_HEADS, HEAD_DIM)],
        axis=2,
    )
    shares = keyval.reshape(tok_rows, head_count, 2 * KV_HEADS * HEAD_DIM // head_count)
    query_local, pairs_local = sent_together((query_send, shares), "head", 1, 0, 2)
    pairs_local = pairs_local.reshape(span_len, -1)
    for level in range(sharers.bit_length() - 1):
        other_half = from_partner(pairs_local, "head", level)
        lower_half = head_index >> level & 1 == 0
        pairs_local = jnp.where(
            lower_half,
            jnp.concatenate([pairs_local, other_half], 1),
            jnp.concatenate([other_half, pairs_local], 1),
        )
    query_local = query_local.reshape(span_len, heads_here, HEAD_DIM)
    grad_local = out_grad.reshape(span_len, heads_here, HEAD_DIM)
    earlier = passed_along(pairs_local[span_len - HALO :], "span", 1)
    extended = jnp.concatenate([earlier, pairs_local], 0)
    base_row = span_index * span_len
    doc_starts = jnp.cumsum(doc_lengths) - doc_lengths
    query_pos = base_row + jnp.arange(span_len, dtype=jnp.int32)
    doc_first = jnp.max(
        jnp.where(doc_starts[None, :] <= query_pos[:, None], doc_starts[None, :], 0), axis=1
    )
    n_blocks = span_len // BLOCK
    per_group = min(n_blocks, max(1, 512 // BLOCK))
    n_groups = n_blocks // per_group
    group_rows = per_group * BLOCK
    width = WINDOW * BLOCK
    block_offsets = jnp.arange(BLOCK, dtype=jnp.int32)
    window_offsets = jnp.arange(width, dtype=jnp.int32)
    block_starts = jnp.arange(per_group, dtype=jnp.int32) * BLOCK

    def attend(gradients, group_index):
        first_row = group_index * group_rows
        query_group = lax.dynamic_slice_in_dim(query_local, first_row, group_rows, 0).reshape(
            per_group, BLOCK, heads_here, HEAD_DIM
        )
        grad_group = lax.dynamic_slice_in_dim(grad_local, first_row, group_rows, 0).reshape(
            per_group, BLOCK, heads_here, HEAD_DIM
        )
        pair_rows = lax.dynamic_slice_in_dim(extended, first_row, group_rows + HALO, 0).reshape(
            per_group + WINDOW - 1, BLOCK, 2 * HEAD_DIM
        )
        window = jnp.stack(
            [pair_rows[shift_index : shift_index + per_group] for shift_index in range(WINDOW)],
            axis=1,
        ).reshape(per_group, width, 2 * HEAD_DIM)
        key_window = window[..., :HEAD_DIM]
        value_window = window[..., HEAD_DIM:]
        query_rows = base_row + first_row + block_starts[:, None] + block_offsets[None, :]
        key_rows = base_row + first_row - HALO + block_starts[:, None] + window_offsets[None, :]
        first_doc = lax.dynamic_slice_in_dim(doc_first, first_row, group_rows, 0).reshape(
            per_group, BLOCK
        )
        allowed = (key_rows[:, None, :] >= first_doc[:, :, None]) & (
            key_rows[:, None, :] <= query_rows[:, :, None]
        )
        scores = (
            jnp.einsum(
                "gqhd,gkd->ghqk", query_group, key_window, preferred_element_type=jnp.float32
            )
            * score_scale
        )
        scores = jnp.where(allowed[:, None], scores, -1e30)
        row_max = jnp.max(scores, axis=-1, keepdims=True)
        exponent = jnp.exp(scores - row_max)
        row_total = jnp.sum(exponent, axis=-1, keepdims=True)
        weights = exponent / row_total
        log_totals = (row_max + jnp.log(row_total))[..., 0]
        weights_low = weights.astype(jnp.bfloat16)
        attention = jnp.einsum(
            "ghqk,gkd->gqhd", weights_low, value_window, preferred_element_type=jnp.float32
        ).astype(jnp.bfloat16)
        attention = lax.optimization_barrier(attention).astype(jnp.float32)
        dweights = jnp.einsum(
            "gqhd,gkd->ghqk", grad_group, value_window, preferred_element_type=jnp.float32
        )
        delta_rows = jnp.einsum("gqhd,gqhd->ghq", grad_group.astype(jnp.float32), attention)
        dscores = (weights * (dweights - delta_rows[..., None])).astype(jnp.bfloat16)
        key_part = (
            jnp.einsum("ghqk,gqhd->gkd", dscores, query_group, preferred_element_type=jnp.float32)
            * score_scale
        )
        value_part = jnp.einsum(
            "ghqk,gqhd->gkd", weights_low, grad_group, preferred_element_type=jnp.float32
        )
        pieces = jnp.concatenate([key_part, value_part], -1).reshape(
            per_group, WINDOW, BLOCK, 2 * HEAD_DIM
        )
        folded = jnp.zeros((per_group + WINDOW - 1, BLOCK, 2 * HEAD_DIM), jnp.float32)
        for shift_index in range(WINDOW):
            folded = folded.at[shift_index : shift_index + per_group].add(pieces[:, shift_index])
        folded = folded.reshape(group_rows + HALO, 2 * HEAD_DIM)
        current = lax.dynamic_slice_in_dim(gradients, first_row, group_rows + HALO, 0)
        gradients = lax.dynamic_update_slice_in_dim(gradients, current + folded, first_row, 0)
        return (gradients, jnp.transpose(log_totals, (1, 0, 2)).reshape(heads_here, group_rows))

    gradients, total_groups = lax.scan(
        attend,
        jnp.zeros((HALO + span_len, 2 * HEAD_DIM), jnp.float32),
        jnp.arange(n_groups, dtype=jnp.int32),
    )
    log_totals = jnp.transpose(total_groups, (1, 0, 2)).reshape(heads_here, span_len)
    returned = passed_along(gradients[:HALO].astype(jnp.bfloat16), "span", -1).astype(jnp.float32)
    local_grads = gradients[HALO:].at[span_len - HALO :].add(returned)
    local_grads = group_total(local_grads.T, sharers, head_index)
    return (local_grads.astype(jnp.bfloat16), log_totals)


def solution(mesh):
    return jax.shard_map(
        shards,
        mesh=mesh,
        in_specs=(
            P(("rep", "span", "head"), None),
            P(("rep", "span", "head"), None),
            P(("rep", "span", "head"), None),
            P(("rep", "span"), "head"),
            P("rep"),
        ),
        out_specs=(P("head", ("rep", "span")), P("head", ("rep", "span"))),
        check_vma=False,
    )
```

profile of v0, /device:TPU:56, one launch (start us, length us, event | category | flops | bytes accessed | tf_op | source)
XLA Modules:
  0.0 219.1 jit_solution(5404256168581891633)
XLA Ops:
  0.7 1.7 copy.101
  2.7 82.5 %all_to_all.18 = bf16[128,16,320]{0,2,1:T(8,128)(2,1)S(1)} all-to-all(bf16[128,16,320]{0,2,1:T(8,128)(2,1)S(1)} %pad_maximum_fusion.2), channel_id=1, replica_groups=mesh['span'=16,'head'=16,'rep'=4] {'head'}, dimensions={1} | all-to-all | bytes 2621440 | tf_op jit(solution)/shard_map/all_to_all | solution.py:34
  85.4 4.1 %collective-permute-start = (bf16[2048,64]{0,1:T(8,128)(2,1)S(1)}, bf16[2048,64]{0,1:T(8,128)(2,1)S(1)}, u32[]{:S(2)}, u32[]{:S(2)}) collective-permute-start(bf16[2048,64]{0,1:T(8,128)(2,1)S(1)} %slice_bitcast_fusion.6), channel_id=1, source_target_pairs={{0,4},{4,0},{8,12},{12,8},{16,20},{20,16},{24,28},{28,24},{32,36},... | collective-permute-start | bytes 786440 | tf_op jit(solution)/shard_map/ppermute | solution.py:23
  89.6 4.3 %collective-permute-done = bf16[2048,64]{0,1:T(8,128)(2,1)S(1)} collective-permute-done((bf16[2048,64]{0,1:T(8,128)(2,1)S(1)}, bf16[2048,64]{0,1:T(8,128)(2,1)S(1)}, u32[]{:S(2)}, u32[]{:S(2)}) %collective-permute-start) | collective-permute-done | bytes 262176 | tf_op jit(solution)/shard_map/ppermute | solution.py:23
  94.0 4.0 %collective-permute-start.1 = (bf16[2048,128]{0,1:T(8,128)(2,1)S(1)}, bf16[2048,128]{0,1:T(8,128)(2,1)S(1)}, u32[]{:S(2)}, u32[]{:S(2)}) collective-permute-start(bf16[2048,128]{0,1:T(8,128)(2,1)S(1)} %maximum_select_fusion.1), channel_id=1, source_target_pairs={{0,8},{8,0},{4,12},{12,4},{16,24},{24,16},{20,28},{28,20},{32,40},... | collective-permute-start | bytes 1572872 | tf_op jit(solution)/shard_map/ppermute | solution.py:23
  98.3 1.4 copy.105
  99.7 19.4 %collective-permute-done.1 = bf16[2048,128]{0,1:T(8,128)(2,1)S(1)} collective-permute-done((bf16[2048,128]{0,1:T(8,128)(2,1)S(1)}, bf16[2048,128]{0,1:T(8,128)(2,1)S(1)}, u32[]{:S(2)}, u32[]{:S(2)}) %collective-permute-start.1) | collective-permute-done | bytes 524320 | tf_op jit(solution)/shard_map/ppermute | solution.py:23
  119.4 1.9 collective-permute-start.2
  122.5 2.5 %collective-permute-done.2 = bf16[128,256]{0,1:T(8,128)(2,1)S(1)} collective-permute-done((bf16[128,256]{0,1:T(8,128)(2,1)S(1)}, bf16[128,256]{0,1:T(8,128)(2,1)S(1)}, u32[]{:S(2)}, u32[]{:S(2)}) %collective-permute-start.2) | collective-permute-done | bytes 65568 | tf_op jit(solution)/shard_map/ppermute | solution.py:44
  125.0 1.1 pad_maximum_fusion.3
  126.1 1.5 broadcast_in_dim.56.clone
  127.6 46.9 %while.19 = (s32[]{:T(128)}, f32[2176,256]{0,1:T(8,128)}, f32[4,2,512]{2,1,0:T(2,128)}, s32[4]{0:T(128)S(1)}, s32[]{:T(128)}, /*index=5*/s32[2048]{0:T(1024)S(1)...) while((s32[]{:T(128)}, f32[2176,256]{0,1:T(8,128)}, ...), condition=%wide.region_5.6_spmd.clone.clone, body=%wide.region_2.5_spmd.clone.clone.sunk | while | flops 340819488 | bytes 33622904 | solution.py:169
  128.9 1.1 constant_dynamic-slice_fusion.10
  136.1 1.1 constant_dynamic-slice_fusion.8
  140.6 1.1 constant_dynamic-slice_fusion.10
  147.8 1.1 constant_dynamic-slice_fusion.8
  159.5 1.1 constant_dynamic-slice_fusion.8
  171.2 1.1 constant_dynamic-slice_fusion.8
  175.4 1.9 collective-permute-start.3
  177.3 1.7 slice.132
  180.2 1.9 collective-permute-start.4
  182.2 26.3 %collective-permute-done.4 = bf16[128,2048]{1,0:T(8,128)(2,1)S(1)} collective-permute-done((bf16[128,2048]{1,0:T(8,128)(2,1)S(1)}, bf16[128,2048]{1,0:T(8,128)(2,1)S(1)}, u32[]{:S(2)}, u32[]{:S(2)}) %collective-permute-start.4) | collective-permute-done | bytes 524320 | tf_op jit(solution)/shard_map/ppermute | solution.py:23
  208.7 1.9 collective-permute-start.5
  210.6 7.7 %collective-permute-done.5 = bf16[64,2048]{1,0:T(8,128)(2,1)S(1)} collective-permute-done((bf16[64,2048]{1,0:T(8,128)(2,1)S(1)}, bf16[64,2048]{1,0:T(8,128)(2,1)S(1)}, u32[]{:S(2)}, u32[]{:S(2)}) %collective-permute-start.5) | collective-permute-done | bytes 262176 | tf_op jit(solution)/shard_map/ppermute | solution.py:23
  (163 shorter events, 42.3 us)
Async XLA Ops:
  0.6 1.7 copy-start.1
  0.6 1.8 copy-start.2
  85.2 12.8 %copy-start.3 = (s32[32]{0:T(128)S(1)}, s32[32]{0:T(128)}, u32[]{:S(2)}) copy-start(s32[32]{0:T(128)} %param.17) | copy-start | bytes 388
  85.2 13.1 %copy-start = (bf16[2048,256]{1,0:T(8,128)(2,1)S(1)}, bf16[2048,256]{1,0:T(8,128)(2,1)}, u32[]{:S(2)}) copy-start(bf16[2048,256]{1,0:T(8,128)(2,1)} %param.16) | copy-start | bytes 3145732
  85.4 8.5 %collective-permute-start = (bf16[2048,64]{0,1:T(8,128)(2,1)S(1)}, bf16[2048,64]{0,1:T(8,128)(2,1)S(1)}, u32[]{:S(2)}, u32[]{:S(2)}) collective-permute-start(bf16[2048,64]{0,1:T(8,128)(2,1)S(1)} %slice_bitcast_fusion.6), channel_id=1, source_target_pairs={{0,4},{4,0},{8,12},{12,8},{16,20},{20,16},{24,28},{28,24},{32,36},... | collective-permute-start | bytes 786440 | tf_op jit(solution)/shard_map/ppermute | solution.py:23
  94.0 25.1 %collective-permute-start.1 = (bf16[2048,128]{0,1:T(8,128)(2,1)S(1)}, bf16[2048,128]{0,1:T(8,128)(2,1)S(1)}, u32[]{:S(2)}, u32[]{:S(2)}) collective-permute-start(bf16[2048,128]{0,1:T(8,128)(2,1)S(1)} %maximum_select_fusion.1), channel_id=1, source_target_pairs={{0,8},{8,0},{4,12},{12,4},{16,24},{24,16},{20,28},{28,20},{32,40},... | collective-permute-start | bytes 1572872 | tf_op jit(solution)/shard_map/ppermute | solution.py:23
  119.4 5.6 %collective-permute-start.2 = (bf16[128,256]{0,1:T(8,128)(2,1)S(1)}, bf16[128,256]{0,1:T(8,128)(2,1)S(1)}, u32[]{:S(2)}, u32[]{:S(2)}) collective-permute-start(bf16[128,256]{0,1:T(8,128)(2,1)S(1)} %slice.157), channel_id=1, source_target_pairs={{0,64},{64,128},{128,192},{192,256},{256,320},{320,384},{384,448},... | collective-permute-start | bytes 196616 | tf_op jit(solution)/shard_map/ppermute | solution.py:44
  175.4 3.8 %collective-permute-start.3 = (bf16[128,256]{0,1:T(8,128)(2,1)S(1)}, bf16[128,256]{0,1:T(8,128)(2,1)S(1)}, u32[]{:S(2)}, u32[]{:S(2)}) collective-permute-start(bf16[128,256]{0,1:T(8,128)(2,1)S(1)} %slice.180), channel_id=1, source_target_pairs={{64,0},{128,64},{192,128},{256,192},{320,256},{384,320},{448,384},... | collective-permute-start | bytes 196616 | tf_op jit(solution)/shard_map/ppermute | solution.py:44
  180.2 28.2 %collective-permute-start.4 = (bf16[128,2048]{1,0:T(8,128)(2,1)S(1)}, bf16[128,2048]{1,0:T(8,128)(2,1)S(1)}, u32[]{:S(2)}, u32[]{:S(2)}) collective-permute-start(bf16[128,2048]{1,0:T(8,128)(2,1)S(1)} %select_convert_fusion), channel_id=1, source_target_pairs={{0,8},{8,0},{4,12},{12,4},{16,24},{24,16},{20,28},{28,20},{32,40},... | collective-permute-start | bytes 1572872 | tf_op jit(solution)/shard_map/ppermute | solution.py:23
  208.7 9.6 %collective-permute-start.5 = (bf16[64,2048]{1,0:T(8,128)(2,1)S(1)}, bf16[64,2048]{1,0:T(8,128)(2,1)S(1)}, u32[]{:S(2)}, u32[]{:S(2)}) collective-permute-start(bf16[64,2048]{1,0:T(8,128)(2,1)S(1)} %select_convert_fusion.1), channel_id=1, source_target_pairs={{0,4},{4,0},{8,12},{12,8},{16,20},{20,16},{24,28},{28,24},{32,36},... | collective-permute-start | bytes 786440 | tf_op jit(solution)/shard_map/ppermute | solution.py:23
where the time goes:
time: 221 us; the launch traced here: 219 us
  blocking collectives  82.5 us (37%)
  waiting for transfers between devices  60.3 us (27%)
  local copies, waits for them, and re-layouts  39.9 us (18%)
  starting transfers between devices  15.8 us (7%)
  other arithmetic  10.7 us (5%)
  matrix products  5.71 us (3%)
  loops' own time  3.3 us (1%)
    all_to_all x1, blocking collectives, sent_together(): lax.all_to_all(both, axis, split_axis=split_dim, concat_axis=concat_dim,...  82.5 us
    ppermute x4, waiting for transfers between devices, from_partner(): return lax.ppermute(block, axis, route)  57.7 us
    ppermute x4, starting transfers between devices, from_partner(): return lax.ppermute(block, axis, route)  12 us
    dynamic_slice x8, local copies, waits for them, and re-layouts, attend(): lax.dynamic_slice_in_dim(gradients, first_row, group_rows + HALO, 0)  5.47 us
    dynamic_slice x8, local copies, waits for them, and re-layouts, attend(): lax.dynamic_slice_in_dim(grad_local, first_row, group_rows, 0)  4.98 us
    dynamic_update_slice x8, local copies, waits for them, and re-layouts, attend(): lax.dynamic_update_slice_in_dim(gradients, current + folded, first_row, 0)  4.62 us
  transfers between devices with their start and end apart: 6, of which 6 were waited for; matrix products, arithmetic and copies ran while one was open for 2% of the time, Pallas kernels for 0%

commit v1 on v0

v1 whole, which is shorter than its diff:
```python
import math

import jax
import jax.numpy as jnp
from jax import lax
from jax.experimental import pallas as pl
from jax.experimental.pallas import tpu as pltpu
from jax.sharding import PartitionSpec as P

HEADS = 32
KV_HEADS = 4
GROUP = HEADS // KV_HEADS
HEAD_DIM = 128
BLOCK = 128
WIDTH = 2 * BLOCK
DOCS = 32
OWNERS = 16
OWNED = 2 * KV_HEADS * HEAD_DIM // OWNERS
HEADS_OWNED = HEADS // OWNERS
EXTRA = 8
SCALE = 1.0 / math.sqrt(HEAD_DIM)
NEG = -1e30
VMEM = pl.BlockSpec(memory_space=pltpu.VMEM)
SMEM = pl.BlockSpec(memory_space=pltpu.SMEM)
NT = (((1,), (1,)), ((), ()))


def dot(a, b, dims=(((1,), (0,)), ((), ()))):
    return lax.dot_general(a, b, dims, preferred_element_type=jnp.float32)


def head_cols(h):
    return slice(h * HEAD_DIM, (h + 1) * HEAD_DIM)


def forward_kernel(base_ref, doc_ref, q_ref, k_ref, k_prev_ref, p_ref, total_ref):
    base = base_ref[0]
    query_pos = base + lax.broadcasted_iota(jnp.int32, (1, BLOCK), 1)
    doc_first = jnp.zeros((1, BLOCK), jnp.int32)
    start = jnp.int32(0)
    for d in range(DOCS):
        doc_first = jnp.where(start <= query_pos, start, doc_first)
        start = start + doc_ref[d]
    key_pos = base - BLOCK + lax.broadcasted_iota(jnp.int32, (WIDTH, BLOCK), 0)
    allowed = (key_pos >= doc_first) & (key_pos <= query_pos)
    bias = jnp.where(allowed, 0.0, NEG)
    for g in range(KV_HEADS):
        keys = jnp.concatenate([k_prev_ref[:, head_cols(g)], k_ref[:, head_cols(g)]], 0)
        for h in range(GROUP):
            head = g * GROUP + h
            s = dot(keys, q_ref[:, head_cols(head)], NT) * (SCALE * math.log2(math.e)) + bias
            row_max = jnp.max(s, axis=0, keepdims=True)
            e = jnp.exp2(s - row_max)
            total = jnp.sum(e, axis=0, keepdims=True)
            p_ref[g, :, head_cols(h)] = (e * (1.0 / total)).astype(jnp.bfloat16)
            total_ref[head : head + 1, :] = (row_max + jnp.log2(total)) * math.log(2.0)


def backward_kernel(p_ref, og_ref, q_ref, v_ref, v_prev_ref, own_ref, halo_ref, ds_ref):
    for g in range(KV_HEADS):
        vals = jnp.concatenate([v_prev_ref[:, head_cols(g)], v_ref[:, head_cols(g)]], 0)
        grads = []
        for h in range(GROUP):
            head = g * GROUP + h
            og = og_ref[head // HEADS_OWNED, :, head_cols(head % HEADS_OWNED)]
            grads.append(og)
            dp = dot(vals, og, NT)
            p = p_ref[g, :, head_cols(h)].astype(jnp.float32)
            delta = jnp.sum(p * dp, axis=0, keepdims=True)
            ds_ref[:, head_cols(h)] = (p * (dp - delta)).astype(jnp.bfloat16)
        queries = jnp.concatenate(
            [q_ref[:, head_cols(g * GROUP + h)] for h in range(GROUP)], 0
        )
        dk = (dot(ds_ref[...], queries) * SCALE).T
        dv = dot(p_ref[g], jnp.concatenate(grads, 0)).T
        for i, grad in enumerate((dk, dv)):
            rows = slice((2 * g + i) * HEAD_DIM, (2 * g + i + 1) * HEAD_DIM)
            halo_ref[rows, :] = grad[:, :BLOCK].astype(jnp.bfloat16)
            own_ref[rows, :] = grad[:, BLOCK:]


def sum_kernel(own_ref, halo_ref, total_ref, send_ref):
    for z in range(OWNERS):
        rows = slice(z * OWNED, (z + 1) * OWNED)
        send_ref[z, :OWNED, :] = (
            own_ref[rows, :] + halo_ref[rows, :].astype(jnp.float32)
        ).astype(jnp.bfloat16)
        total = total_ref[z * HEADS_OWNED : (z + 1) * HEADS_OWNED, :]
        high = total.astype(jnp.bfloat16).astype(jnp.float32)
        low = total - high
        pad = jnp.zeros((EXTRA - 2 * HEADS_OWNED, BLOCK), jnp.float32)
        send_ref[z, OWNED:, :] = jnp.concatenate([high, low, pad], 0).astype(jnp.bfloat16)


def unpack_kernel(got_ref, grads_ref, total_ref):
    for b in range(OWNERS):
        cols = slice(b * BLOCK, (b + 1) * BLOCK)
        grads_ref[:, cols] = got_ref[b, :OWNED, :]
        extra = got_ref[b, OWNED:, :].astype(jnp.float32)
        total_ref[:, cols] = extra[:HEADS_OWNED] + extra[HEADS_OWNED : 2 * HEADS_OWNED]


def call(kernel, out_shape, args, specs, scratch=(), flops=0, exps=0):
    outs = jax.tree.leaves(out_shape)
    moved = sum(math.prod(a.shape) * a.dtype.itemsize for a in [*args, *outs])
    return pl.pallas_call(
        kernel,
        out_shape=out_shape,
        in_specs=specs,
        out_specs=jax.tree.map(lambda _: VMEM, out_shape),
        scratch_shapes=scratch,
        compiler_params=pltpu.CompilerParams(vmem_limit_bytes=40 * 2**20),
        cost_estimate=pl.CostEstimate(
            flops=flops, bytes_accessed=moved, transcendentals=exps
        ),
    )(*args)


def shards(queries, keys, values, out_grad, doc_lengths):
    spans, owners = lax.axis_size("span"), lax.axis_size("head")
    block_index = lax.axis_index("span") * owners + lax.axis_index("head")
    blocks = spans * owners
    base = jnp.full((1,), block_index * BLOCK, jnp.int32)
    f32, bf16 = jnp.float32, jnp.bfloat16
    onward = [(i, i + 1) for i in range(blocks - 1)]
    back = [(i + 1, i) for i in range(blocks - 1)]
    og = lax.all_to_all(
        out_grad.reshape(owners, BLOCK, HEADS_OWNED * HEAD_DIM), "head", 0, 0, tiled=True
    )
    k_prev = lax.ppermute(keys, ("span", "head"), onward)
    v_prev = lax.ppermute(values, ("span", "head"), onward)
    macs = HEADS * BLOCK * WIDTH * HEAD_DIM
    weights, totals = call(
        forward_kernel,
        (
            jax.ShapeDtypeStruct((KV_HEADS, WIDTH, GROUP * BLOCK), bf16),
            jax.ShapeDtypeStruct((HEADS, BLOCK), f32),
        ),
        (base, doc_lengths, queries, keys, k_prev),
        [SMEM, SMEM, VMEM, VMEM, VMEM],
        flops=2 * macs,
        exps=HEADS * BLOCK * WIDTH,
    )
    features = 2 * KV_HEADS * HEAD_DIM
    own, halo = call(
        backward_kernel,
        (
            jax.ShapeDtypeStruct((features, BLOCK), f32),
            jax.ShapeDtypeStruct((features, BLOCK), bf16),
        ),
        (weights, og, queries, values, v_prev),
        [VMEM] * 5,
        scratch=[pltpu.VMEM((WIDTH, GROUP * BLOCK), bf16)],
        flops=6 * macs,
    )
    returned = lax.ppermute(halo, ("span", "head"), back)
    send = call(
        sum_kernel,
        jax.ShapeDtypeStruct((owners, OWNED + EXTRA, BLOCK), bf16),
        (own, returned, totals),
        [VMEM] * 3,
    )
    got = lax.all_to_all(send, "head", 0, 0, tiled=True)
    return call(
        unpack_kernel,
        (
            jax.ShapeDtypeStruct((OWNED, owners * BLOCK), bf16),
            jax.ShapeDtypeStruct((HEADS_OWNED, owners * BLOCK), f32),
        ),
        (got,),
        [VMEM],
    )


def solution(mesh):
    return jax.shard_map(
        shards,
        mesh=mesh,
        in_specs=(
            P(("rep", "span", "head"), None),
            P(("rep", "span", "head"), None),
            P(("rep", "span", "head"), None),
            P(("rep", "span"), "head"),
            P("rep"),
        ),
        out_specs=(P("head", ("rep", "span")), P("head", ("rep", "span"))),
        check_vma=False,
    )
```

time: 221 us -> 121 us (0.55)
  blocking collectives: 82.5 us -> 31 us
  local copies, waits for them, and re-layouts: 39.9 us -> 4.67 us
  starting transfers between devices: 15.8 us -> 29.6 us
  waiting for transfers between devices: 60.3 us -> 48.2 us
  other arithmetic: 10.7 us -> 0 us
  Pallas kernels: 0 us -> 6.49 us
  matrix products: 5.71 us -> 0 us
  loops' own time: 3.3 us -> 0 us
    all_to_all x1, blocking collectives: 82.5 us -> 31 us  [shards(): got = lax.all_to_all(send, 'head', 0, 0, tiled=True)]
    all_to_all x0 -> x1, starting transfers between devices: none -> 19 us  [shards(): lax.all_to_all(out_grad.reshape(owners, BLOCK, HEADS_OWNED * HEAD_DIM), '...]
    dynamic_slice x24 -> x0, local copies, waits for them, and re-layouts: 13.5 us -> none  [the longest x8 5.47 us: attend(): lax.dynamic_slice_in_dim(gradients, first_row, group_rows + HALO, 0)]
    ppermute x6 -> x3, waiting for transfers between devices: 60.3 us -> 48.2 us  [the longest x1 43 us: shards(): k_prev = lax.ppermute(keys, ('span', 'head'), onward)]
    slice x11 -> x0, local copies, waits for them, and re-layouts: 10.3 us -> none  [the longest x4 4.38 us: attend(): pair_rows[shift_index:shift_index + per_group]]
    pallas_call x0 -> x4, Pallas kernels: none -> 6.49 us  [call(): pl.pallas_call(kernel, out_shape=out_shape, in_specs=specs, out_specs=jax...]
    dot_general x16 -> x0, matrix products: 5.71 us -> none  [the longest x4 2.06 us: attend(): jnp.einsum('ghqk,gqhd->gkd', dscores, query_group, preferred_element_type...]
    ppermute x6 -> x3, starting transfers between devices: 15.8 us -> 10.6 us  [the longest x1 3.83 us: shards(): k_prev = lax.ppermute(keys, ('span', 'head'), onward)]
  transfers between devices with their start and end apart: 6 -> 4, of which waited for: 6 -> 2; matrix products, arithmetic and copies ran while one was open for 2% -> 0% of each run, Pallas kernels for 0% -> 2%
where the time goes in v1:
time: 121 us
  waiting for transfers between devices  48.2 us (40%)
  blocking collectives  31 us (26%)
  starting transfers between devices  29.6 us (24%)
  Pallas kernels  6.49 us (5%)
  local copies, waits for them, and re-layouts  4.67 us (4%)
    ppermute x1, waiting for transfers between devices, shards(): k_prev = lax.ppermute(keys, ('span', 'head'), onward)  43 us
    all_to_all x1, blocking collectives, shards(): got = lax.all_to_all(send, 'head', 0, 0, tiled=True)  31 us
    all_to_all x1, starting transfers between devices, shards(): lax.all_to_all(out_grad.reshape(owners, BLOCK, HEADS_OWNED * HEAD_DIM), '...  19 us
    pallas_call x4, Pallas kernels, call(): pl.pallas_call(kernel, out_shape=out_shape, in_specs=specs, out_specs=jax...  6.49 us
    ppermute x1, waiting for transfers between devices, shards(): returned = lax.ppermute(halo, ('span', 'head'), back)  5.18 us
    unnamed x14, local copies, waits for them, and re-layouts  4.67 us
    ppermute x1, starting transfers between devices, shards(): k_prev = lax.ppermute(keys, ('span', 'head'), onward)  3.83 us
    ppermute x1, starting transfers between devices, shards(): returned = lax.ppermute(halo, ('span', 'head'), back)  3.38 us
  transfers between devices with their start and end apart: 4, of which 2 were waited for; matrix products, arithmetic and copies ran while one was open for 0% of the time, Pallas kernels for 2%

profile of v1, /device:TPU:56, one launch (start us, length us, event | category | flops | bytes accessed | tf_op | source)
XLA Modules:
  0.0 120.6 jit_solution(5665740568085814032)
XLA Ops:
  0.6 0.0 copy-start.3
  0.6 0.0 copy-start.2
  0.6 19.0 %all-to-all-start = ((bf16[16,128,256]{2,1,0:T(8,128)(2,1)}), bf16[16,128,256]{2,1,0:T(8,128)(2,1)S(1)}, u32[]{:S(2)}, u32[]{:S(2)}) async-start(bf16[16,128,256]{2,1,0:T(8,128)(2,1)} %bitcast.2), calls=%async_computation | async-start | bytes 2097152 | tf_op jit(solution)/shard_map/all_to_all | solution.py:127
  19.7 0.0 copy-done.3
  19.7 3.8 %collective-permute-start = (bf16[128,512]{1,0:T(8,128)(2,1)S(1)}, bf16[128,512]{1,0:T(8,128)(2,1)S(1)}, u32[]{:S(2)}, u32[]{:S(2)}) collective-permute-start(bf16[128,512]{1,0:T(8,128)(2,1)S(1)} %copy-done.3), channel_id=1, source_target_pairs={{0,4},{4,8},{8,12},{12,16},{16,20},{20,24},{24,28},{28,32},{32,36}... | collective-permute-start | bytes 393224 | tf_op jit(solution)/shard_map/ppermute | solution.py:130
  23.5 0.0 copy-done.2
  23.5 3.4 %collective-permute-start.1 = (bf16[128,512]{1,0:T(8,128)(2,1)S(1)}, bf16[128,512]{1,0:T(8,128)(2,1)S(1)}, u32[]{:S(2)}, u32[]{:S(2)}) collective-permute-start(bf16[128,512]{1,0:T(8,128)(2,1)S(1)} %copy-done.2), channel_id=1, source_target_pairs={{0,4},{4,8},{8,12},{12,16},{16,20},{20,24},{24,28},{28,32},{32,36}... | collective-permute-start | bytes 393224 | tf_op jit(solution)/shard_map/ppermute | solution.py:131
  26.9 43.0 %collective-permute-done.k_prev_ref = bf16[128,512]{1,0:T(8,128)(2,1)S(1)} collective-permute-done((bf16[128,512]{1,0:T(8,128)(2,1)S(1)}, bf16[128,512]{1,0:T(8,128)(2,1)S(1)}, u32[]{:S(2)}, u32[]{:S(2)}) %collective-permute-start) | collective-permute-done | bytes 131104 | tf_op jit(solution)/shard_map/ppermute | solution.py:130
  69.9 0.0 copy-start.4
  69.9 0.7 copy-done.4
  70.6 1.2 %copy-done = bf16[128,4096]{1,0:T(8,128)(2,1)S(1)} copy-done((bf16[128,4096]{1,0:T(8,128)(2,1)S(1)}, bf16[128,4096]{1,0:T(8,128)(2,1)}, u32[]{:S(2)}) %copy-start) | copy-done | bytes 1048600
  71.8 0.9 copy-done.5
  72.7 0.7 copy-done.6
  73.4 2.6 %shard_map.68 = (bf16[4,256,1024]{2,1,0:T(8,128)(2,1)S(1)}, f32[32,128]{1,0:T(8,128)S(1)}) custom-call(s32[1]{0:T(128)} %bitcast.base_ref, s32[32]{0:T(128)S(1)} %copy-done.6, bf16[128,4096]{1,0:T(8,128)(2,1)S(1)} %copy-done, bf16[128,512]{1,0:T(8,128)(2,1)S(1)} %copy-done.3, bf16[128,512]{1,0:T(8,128)(2,1)S(1)} %copy-done.5), custom_call_target="tpu_custom_call" | custom-call | flops 268435456 | bytes 3424388 | tf_op jit(solution)/shard_map/pallas_call | solution.py:106
  75.9 0.0 collective-permute-done.1.v_prev_ref
  76.0 0.0 all-to-all-done.og_ref
  76.0 0.0 copy-start.1
  76.0 1.2 %copy-done.1 = bf16[128,4096]{1,0:T(8,128)(2,1)S(1)} copy-done((bf16[128,4096]{1,0:T(8,128)(2,1)S(1)}, bf16[128,4096]{1,0:T(8,128)(2,1)}, u32[]{:S(2)}) %copy-start.1) | copy-done | bytes 1048600
  77.2 3.1 %shard_map.69 = (f32[1024,128]{1,0:T(8,128)S(1)}, bf16[1024,128]{1,0:T(8,128)(2,1)S(1)}) custom-call(bf16[4,256,1024]{2,1,0:T(8,128)(2,1)S(1)} %get-tuple-element.6.p_ref, bf16[16,128,256]{2,1,0:T(8,128)(2,1)S(1)} %all-to-all-done.og_ref, bf16[128,4096]{1,0:T(8,128)(2,1)S(1)} %copy-done.1, bf16[128,512]{1,0:T(8,128)(2,1)S(1)} %copy-done.2, ...), custom_call_target="tpu_custom_call" | custom-call | flops 805306368 | bytes 5242880 | tf_op jit(solution)/shard_map/pallas_call | solution.py:106
  80.3 3.4 %collective-permute-start.2 = (bf16[1024,128]{1,0:T(8,128)(2,1)S(1)}, bf16[1024,128]{1,0:T(8,128)(2,1)S(1)}, u32[]{:S(2)}, u32[]{:S(2)}) collective-permute-start(bf16[1024,128]{1,0:T(8,128)(2,1)S(1)} %get-tuple-element.8), channel_id=1, source_target_pairs={{4,0},{8,4},{12,8},{16,12},{20,16},{24,20},{28,24},{32,28},{36,32}... | collective-permute-start | bytes 786440 | tf_op jit(solution)/shard_map/ppermute | solution.py:156
  83.7 5.2 %collective-permute-done.2.halo_ref = bf16[1024,128]{1,0:T(8,128)(2,1)S(1)} collective-permute-done((bf16[1024,128]{1,0:T(8,128)(2,1)S(1)}, bf16[1024,128]{1,0:T(8,128)(2,1)S(1)}, u32[]{:S(2)}, u32[]{:S(2)}) %collective-permute-start.2) | collective-permute-done | bytes 262176 | tf_op jit(solution)/shard_map/ppermute | solution.py:156
  88.9 0.1 shard_map.70
  88.9 31.0 %all_to_all.10.got_ref = bf16[16,72,128]{2,1,0:T(8,128)(2,1)S(1)} all-to-all(bf16[16,72,128]{2,1,0:T(8,128)(2,1)S(1)} %shard_map.70), channel_id=1, replica_groups=mesh['span'=16,'head'=16,'rep'=4] {'head'}, dimensions={0} | all-to-all | bytes 589824 | tf_op jit(solution)/shard_map/all_to_all | solution.py:163
  119.9 0.8 shard_map.71
  (3 shorter events, 0.0 us)
Async XLA Ops:
  0.6 19.0 %copy-start.3 = (bf16[128,512]{1,0:T(8,128)(2,1)S(1)}, bf16[128,512]{1,0:T(8,128)(2,1)}, u32[]{:S(2)}) copy-start(bf16[128,512]{1,0:T(8,128)(2,1)} %k_ref.1) | copy-start | bytes 393220
  0.6 22.9 %copy-start.2 = (bf16[128,512]{1,0:T(8,128)(2,1)S(1)}, bf16[128,512]{1,0:T(8,128)(2,1)}, u32[]{:S(2)}) copy-start(bf16[128,512]{1,0:T(8,128)(2,1)} %v_ref.1) | copy-start | bytes 393220
  0.6 75.3 %all-to-all-start = ((bf16[16,128,256]{2,1,0:T(8,128)(2,1)}), bf16[16,128,256]{2,1,0:T(8,128)(2,1)S(1)}, u32[]{:S(2)}, u32[]{:S(2)}) async-start(bf16[16,128,256]{2,1,0:T(8,128)(2,1)} %bitcast.2), calls=%async_computation | async-start | bytes 2097152 | tf_op jit(solution)/shard_map/all_to_all | solution.py:127
  19.7 50.3 %collective-permute-start = (bf16[128,512]{1,0:T(8,128)(2,1)S(1)}, bf16[128,512]{1,0:T(8,128)(2,1)S(1)}, u32[]{:S(2)}, u32[]{:S(2)}) collective-permute-start(bf16[128,512]{1,0:T(8,128)(2,1)S(1)} %copy-done.3), channel_id=1, source_target_pairs={{0,4},{4,8},{8,12},{12,16},{16,20},{20,24},{24,28},{28,32},{32,36}... | collective-permute-start | bytes 393224 | tf_op jit(solution)/shard_map/ppermute | solution.py:130
  23.5 52.4 %collective-permute-start.1 = (bf16[128,512]{1,0:T(8,128)(2,1)S(1)}, bf16[128,512]{1,0:T(8,128)(2,1)S(1)}, u32[]{:S(2)}, u32[]{:S(2)}) collective-permute-start(bf16[128,512]{1,0:T(8,128)(2,1)S(1)} %copy-done.2), channel_id=1, source_target_pairs={{0,4},{4,8},{8,12},{12,16},{16,20},{20,24},{24,28},{28,32},{32,36}... | collective-permute-start | bytes 393224 | tf_op jit(solution)/shard_map/ppermute | solution.py:131
  69.9 0.7 copy-start.4
  70.6 1.2 %copy-start = (bf16[128,4096]{1,0:T(8,128)(2,1)S(1)}, bf16[128,4096]{1,0:T(8,128)(2,1)}, u32[]{:S(2)}) copy-start(bf16[128,4096]{1,0:T(8,128)(2,1)} %q_ref.3) | copy-start | bytes 3145732
  71.8 0.9 copy-start.5
  72.7 0.7 copy-start.6
  76.0 1.2 %copy-start.1 = (bf16[128,4096]{1,0:T(8,128)(2,1)S(1)}, bf16[128,4096]{1,0:T(8,128)(2,1)}, u32[]{:S(2)}) copy-start(bf16[128,4096]{1,0:T(8,128)(2,1)} %q_ref.3) | copy-start | bytes 3145732
  80.3 8.6 %collective-permute-start.2 = (bf16[1024,128]{1,0:T(8,128)(2,1)S(1)}, bf16[1024,128]{1,0:T(8,128)(2,1)S(1)}, u32[]{:S(2)}, u32[]{:S(2)}) collective-permute-start(bf16[1024,128]{1,0:T(8,128)(2,1)S(1)} %get-tuple-element.8), channel_id=1, source_target_pairs={{4,0},{8,4},{12,8},{16,12},{20,16},{24,20},{28,24},{32,28},{36,32}... | collective-permute-start | bytes 786440 | tf_op jit(solution)/shard_map/ppermute | solution.py:156

commit v2 on v1

v2 whole, which is shorter than its diff:
```python
import math

import jax
import jax.numpy as jnp
from jax import lax
from jax.experimental import pallas as pl
from jax.experimental.pallas import tpu as pltpu
from jax.sharding import PartitionSpec as P

HEADS = 32
KV_HEADS = 4
GROUP = HEADS // KV_HEADS
HEAD_DIM = 128
BLOCK = 128
WIDTH = 2 * BLOCK
DOCS = 32
OWNERS = 16
OWNED = 2 * KV_HEADS * HEAD_DIM // OWNERS
HEADS_OWNED = HEADS // OWNERS
EXTRA = 8
SCALE = 1.0 / math.sqrt(HEAD_DIM)
SCORE_SCALE = SCALE * math.log2(math.e)
NEG = -1e30
PAIRS = GROUP // 2
VMEM = pl.BlockSpec(memory_space=pltpu.VMEM)
SMEM = pl.BlockSpec(memory_space=pltpu.SMEM)
NT = (((1,), (1,)), ((), ()))


def dot(a, b, dims=(((1,), (0,)), ((), ()))):
    return lax.dot_general(a, b, dims, preferred_element_type=jnp.float32)


def pair_rows(ref, pair):
    left = 2 * pair * HEAD_DIM
    return jnp.concatenate(
        [ref[:, left : left + HEAD_DIM], ref[:, left + HEAD_DIM : left + 2 * HEAD_DIM]], 0
    )


def pair_cols(pair):
    return slice(2 * pair * BLOCK, 2 * (pair + 1) * BLOCK)


def twice(x):
    return jnp.concatenate([x, x], 1)


def feature_rows(group, which):
    first = (2 * group + which) * HEAD_DIM
    return slice(first, first + HEAD_DIM)


def head_cols(h):
    return slice(h * HEAD_DIM, (h + 1) * HEAD_DIM)


def own_scores_kernel(
    base_ref, doc_ref, q_ref, k_ref, v_ref, e_ref, stats_ref, bias_ref, q_out_ref, v_out_ref
):
    q_out_ref[...] = q_ref[...]
    v_out_ref[...] = v_ref[...]
    base = base_ref[0]
    query_pos = base + lax.broadcasted_iota(jnp.int32, (1, BLOCK), 1)
    doc_first = jnp.zeros((1, BLOCK), jnp.int32)
    start = jnp.int32(0)
    for d in range(DOCS):
        doc_first = jnp.where(start <= query_pos, start, doc_first)
        start = start + doc_ref[d]
    key_pos = base + lax.broadcasted_iota(jnp.int32, (BLOCK, BLOCK), 0)
    bias_ref[...] = jnp.where(key_pos - BLOCK >= doc_first, 0.0, NEG)
    bias = twice(jnp.where((key_pos >= doc_first) & (key_pos <= query_pos), 0.0, NEG))
    for g in range(KV_HEADS):
        for i in range(PAIRS):
            pair = g * PAIRS + i
            s = dot(k_ref[:, head_cols(g)], pair_rows(q_ref, pair), NT) * SCORE_SCALE + bias
            row_max = jnp.max(s, axis=0, keepdims=True)
            e = jnp.exp2(s - row_max)
            e_ref[g, :, pair_cols(i)] = e
            stats_ref[0, pair : pair + 1, :] = row_max
            stats_ref[1, pair : pair + 1, :] = jnp.sum(e, axis=0, keepdims=True)


def halo_kernel(
    e_ref, stats_ref, bias_ref, q_ref, v_ref, k_far_ref, v_far_ref, og_far_ref,
    halo_ref, p_ref, ds_ref, total_ref, og_ref, p_prev_ref, ds_prev_ref, k_prev_ref, v_prev_ref, sems,
):
    copies = [
        pltpu.make_async_copy(k_far_ref, k_prev_ref, sems.at[KV_HEADS]),
        pltpu.make_async_copy(v_far_ref, v_prev_ref, sems.at[KV_HEADS + 1]),
    ]
    og_copies = [
        pltpu.make_async_copy(
            og_far_ref.at[pl.ds(g * PAIRS, PAIRS)], og_ref.at[pl.ds(g * PAIRS, PAIRS)], sems.at[g]
        )
        for g in range(KV_HEADS)
    ]
    for copy in copies + og_copies:
        copy.start()
    for copy in copies:
        copy.wait()
    bias = twice(bias_ref[...])
    for g in range(KV_HEADS):
        og_copies[g].wait()
        vals = jnp.concatenate([v_prev_ref[:, head_cols(g)], v_ref[:, head_cols(g)]], 0)
        queries, grads = [], []
        for i in range(PAIRS):
            pair = g * PAIRS + i
            q = pair_rows(q_ref, pair)
            og = pair_rows(og_ref.at[pair], 0)
            queries.append(q)
            grads.append(og)
            s = dot(k_prev_ref[:, head_cols(g)], q, NT) * SCORE_SCALE + bias
            own_max = stats_ref[0, pair : pair + 1, :]
            row_max = jnp.maximum(jnp.max(s, axis=0, keepdims=True), own_max)
            e = jnp.exp2(s - row_max)
            shrink = jnp.exp2(own_max - row_max)
            total = jnp.sum(e, axis=0, keepdims=True) + shrink * stats_ref[1, pair : pair + 1, :]
            total_ref[pair : pair + 1, :] = (row_max + jnp.log2(total)) * math.log(2.0)
            inverse = 1.0 / total
            p_prev = e * inverse
            p_own = e_ref[g, :, pair_cols(i)] * (shrink * inverse)
            dp = dot(vals, og, NT)
            dp_prev, dp_own = dp[:BLOCK], dp[BLOCK:]
            delta = jnp.sum(p_prev * dp_prev, axis=0, keepdims=True) + jnp.sum(
                p_own * dp_own, axis=0, keepdims=True
            )
            p_prev_ref[:, pair_cols(i)] = p_prev.astype(jnp.bfloat16)
            ds_prev_ref[:, pair_cols(i)] = (p_prev * (dp_prev - delta)).astype(jnp.bfloat16)
            p_ref[g, :, pair_cols(i)] = p_own.astype(jnp.bfloat16)
            ds_ref[g, :, pair_cols(i)] = (p_own * (dp_own - delta)).astype(jnp.bfloat16)
        dk = dot(ds_prev_ref[...], jnp.concatenate(queries, 0)) * SCALE
        dv = dot(p_prev_ref[...], jnp.concatenate(grads, 0))
        halo_ref[feature_rows(g, 0), :] = dk.T.astype(jnp.bfloat16)
        halo_ref[feature_rows(g, 1), :] = dv.T.astype(jnp.bfloat16)


def own_kernel(p_ref, ds_ref, q_ref, og_ref, own_ref):
    for g in range(KV_HEADS):
        pairs = range(g * PAIRS, (g + 1) * PAIRS)
        queries = jnp.concatenate([pair_rows(q_ref, pair) for pair in pairs], 0)
        grads = jnp.concatenate([pair_rows(og_ref.at[pair], 0) for pair in pairs], 0)
        own_ref[feature_rows(g, 0), :] = (dot(ds_ref[g], queries) * SCALE).T
        own_ref[feature_rows(g, 1), :] = dot(p_ref[g], grads).T


def sum_kernel(own_ref, halo_ref, total_ref, send_ref):
    for z in range(OWNERS):
        rows = slice(z * OWNED, (z + 1) * OWNED)
        send_ref[z, :OWNED, :] = (
            own_ref[rows, :] + halo_ref[rows, :].astype(jnp.float32)
        ).astype(jnp.bfloat16)
        total = total_ref[z : z + 1, :]
        total = jnp.concatenate([total[:, :BLOCK], total[:, BLOCK:]], 0)
        high = total.astype(jnp.bfloat16).astype(jnp.float32)
        low = total - high
        pad = jnp.zeros((EXTRA - 2 * HEADS_OWNED, BLOCK), jnp.float32)
        send_ref[z, OWNED:, :] = jnp.concatenate([high, low, pad], 0).astype(jnp.bfloat16)


def unpack_kernel(got_ref, grads_ref, total_ref):
    for b in range(OWNERS):
        cols = slice(b * BLOCK, (b + 1) * BLOCK)
        grads_ref[:, cols] = got_ref[b, :OWNED, :]
        extra = got_ref[b, OWNED:, :].astype(jnp.float32)
        total_ref[:, cols] = extra[:HEADS_OWNED] + extra[HEADS_OWNED : 2 * HEADS_OWNED]


def call(kernel, out_shape, args, specs, scratch=(), flops=0, exps=0, limit=8):
    outs = jax.tree.leaves(out_shape)
    moved = sum(math.prod(a.shape) * a.dtype.itemsize for a in [*args, *outs])
    return pl.pallas_call(
        kernel,
        out_shape=out_shape,
        in_specs=specs,
        out_specs=jax.tree.map(lambda _: VMEM, out_shape),
        scratch_shapes=scratch,
        compiler_params=pltpu.CompilerParams(vmem_limit_bytes=limit * 2**20),
        cost_estimate=pl.CostEstimate(
            flops=flops, bytes_accessed=moved, transcendentals=exps
        ),
    )(*args)


def shards(queries, keys, values, out_grad, doc_lengths):
    spans, owners = lax.axis_size("span"), lax.axis_size("head")
    block_index = lax.axis_index("span") * owners + lax.axis_index("head")
    blocks = spans * owners
    base = jnp.full((1,), block_index * BLOCK, jnp.int32)
    f32, bf16 = jnp.float32, jnp.bfloat16
    onward = [(i, i + 1) for i in range(blocks - 1)]
    back = [(i + 1, i) for i in range(blocks - 1)]
    og = lax.all_to_all(
        out_grad.reshape(owners, BLOCK, HEADS_OWNED * HEAD_DIM), "head", 0, 0, tiled=True
    )
    k_prev = lax.ppermute(keys, ("span", "head"), onward)
    v_prev = lax.ppermute(values, ("span", "head"), onward)
    macs = HEADS * BLOCK * BLOCK * HEAD_DIM
    array = jax.ShapeDtypeStruct
    exponents, stats, bias, held_queries, held_values = call(
        own_scores_kernel,
        (
            array((KV_HEADS, BLOCK, GROUP * BLOCK), f32),
            array((2, owners, HEADS_OWNED * BLOCK), f32),
            array((BLOCK, BLOCK), f32),
            array(queries.shape, bf16),
            array(values.shape, bf16),
        ),
        (base, doc_lengths, queries, keys, values),
        [SMEM, SMEM] + [VMEM] * 3,
        flops=20000 * macs,
        exps=HEADS * BLOCK * BLOCK,
    )
    features = 2 * KV_HEADS * HEAD_DIM
    kept = array((KV_HEADS, BLOCK, GROUP * BLOCK), bf16)
    halo, weights, dscores, totals, held_grads = call(
        halo_kernel,
        (
            array((features, BLOCK), bf16),
            kept,
            kept,
            array((owners, HEADS_OWNED * BLOCK), f32),
            array(og.shape, bf16),
        ),
        (exponents, stats, bias, held_queries, held_values, k_prev, v_prev, og),
        [VMEM] * 5 + [pl.BlockSpec(memory_space=pl.ANY)] * 3,
        scratch=[pltpu.VMEM((BLOCK, GROUP * BLOCK), bf16)] * 2
        + [pltpu.VMEM(values.shape, bf16)] * 2
        + [pltpu.SemaphoreType.DMA((KV_HEADS + 2,))],
        flops=10 * macs,
        exps=HEADS * BLOCK * BLOCK,
    )
    returned = lax.ppermute(halo, ("span", "head"), back)
    own = call(
        own_kernel,
        array((features, BLOCK), f32),
        (weights, dscores, held_queries, held_grads),
        [VMEM] * 4,
        flops=4 * macs,
    )
    send = call(
        sum_kernel,
        array((owners, OWNED + EXTRA, BLOCK), bf16),
        (own, returned, totals),
        [VMEM] * 3,
    )
    got = lax.all_to_all(send, "head", 0, 0, tiled=True)
    return call(
        unpack_kernel,
        (
            array((OWNED, owners * BLOCK), bf16),
            array((HEADS_OWNED, owners * BLOCK), f32),
        ),
        (got,),
        [VMEM],
    )


def solution(mesh):
    return jax.shard_map(
        shards,
        mesh=mesh,
        in_specs=(
            P(("rep", "span", "head"), None),
            P(("rep", "span", "head"), None),
            P(("rep", "span", "head"), None),
            P(("rep", "span"), "head"),
            P("rep"),
        ),
        out_specs=(P("head", ("rep", "span")), P("head", ("rep", "span"))),
        check_vma=False,
    )
```

time: 121 us -> 118 us (0.975)
  local copies, waits for them, and re-layouts: 4.67 us -> 1.22 us
  blocking collectives: 31 us -> 29.2 us
  Pallas kernels: 6.49 us -> 8.26 us
    ppermute x1, waiting for transfers between devices: 0.01 us -> 3.58 us  [shards(): v_prev = lax.ppermute(values, ('span', 'head'), onward)]
    unnamed x14 -> x4, local copies, waits for them, and re-layouts: 4.67 us -> 1.22 us
    ppermute x1, waiting for transfers between devices: 43 us -> 40 us  [shards(): k_prev = lax.ppermute(keys, ('span', 'head'), onward)]
    pallas_call x4 -> x5, Pallas kernels: 6.49 us -> 8.26 us  [call(): pl.pallas_call(kernel, out_shape=out_shape, in_specs=specs, out_specs=jax...]
    all_to_all x1, blocking collectives: 31 us -> 29.2 us  [shards(): got = lax.all_to_all(send, 'head', 0, 0, tiled=True)]
  transfers between devices with their start and end apart: 4 -> 4, of which waited for: 2 -> 3; matrix products, arithmetic and copies ran while one was open for 0% -> 0% of each run, Pallas kernels for 2% -> 2%
where the time goes in v2:
time: 118 us
  waiting for transfers between devices  49.4 us (42%)
  blocking collectives  29.2 us (25%)
  starting transfers between devices  29.1 us (25%)
  Pallas kernels  8.26 us (7%)
  local copies, waits for them, and re-layouts  1.22 us (1%)
    ppermute x1, waiting for transfers between devices, shards(): k_prev = lax.ppermute(keys, ('span', 'head'), onward)  40 us
    all_to_all x1, blocking collectives, shards(): got = lax.all_to_all(send, 'head', 0, 0, tiled=True)  29.2 us
    all_to_all x1, starting transfers between devices, shards(): lax.all_to_all(out_grad.reshape(owners, BLOCK, HEADS_OWNED * HEAD_DIM), '...  18.9 us
    pallas_call x5, Pallas kernels, call(): pl.pallas_call(kernel, out_shape=out_shape, in_specs=specs, out_specs=jax...  8.26 us
    ppermute x1, waiting for transfers between devices, shards(): returned = lax.ppermute(halo, ('span', 'head'), back)  5.84 us
    ppermute x1, starting transfers between devices, shards(): k_prev = lax.ppermute(keys, ('span', 'head'), onward)  3.77 us
    ppermute x1, waiting for transfers between devices, shards(): v_prev = lax.ppermute(values, ('span', 'head'), onward)  3.58 us
    ppermute x1, starting transfers between devices, shards(): v_prev = lax.ppermute(values, ('span', 'head'), onward)  3.37 us
  transfers between devices with their start and end apart: 4, of which 3 were waited for; matrix products, arithmetic and copies ran while one was open for 0% of the time, Pallas kernels for 2%

profile of v2, /device:TPU:56, one launch (start us, length us, event | category | flops | bytes accessed | tf_op | source)
XLA Modules:
  0.0 118.0 jit_solution(8280604187491799195)
XLA Ops:
  0.6 0.0 copy-start.1
  0.6 18.9 %all-to-all-start = ((bf16[16,128,256]{2,1,0:T(8,128)(2,1)}), bf16[16,128,256]{2,1,0:T(8,128)(2,1)}, u32[]{:S(2)}, u32[]{:S(2)}) async-start(bf16[16,128,256]{2,1,0:T(8,128)(2,1)} %bitcast.2), calls=%async_computation | async-start | bytes 2097152 | tf_op jit(solution)/shard_map/all_to_all | solution.py:193
  19.6 3.8 %collective-permute-start = (bf16[128,512]{1,0:T(8,128)(2,1)}, bf16[128,512]{1,0:T(8,128)(2,1)}, u32[]{:S(2)}, u32[]{:S(2)}) collective-permute-start(bf16[128,512]{1,0:T(8,128)(2,1)} %k_ref.1), channel_id=1, source_target_pairs={{0,4},{4,8},{8,12},{12,16},{16,20},{20,24},{24,28},{28,32},{32,36}... | collective-permute-start | bytes 393224 | tf_op jit(solution)/shard_map/ppermute | solution.py:196
  23.4 3.4 %collective-permute-start.1 = (bf16[128,512]{1,0:T(8,128)(2,1)}, bf16[128,512]{1,0:T(8,128)(2,1)}, u32[]{:S(2)}, u32[]{:S(2)}) collective-permute-start(bf16[128,512]{1,0:T(8,128)(2,1)} %v_ref.1), channel_id=1, source_target_pairs={{0,4},{4,8},{8,12},{12,16},{16,20},{20,24},{24,28},{28,32},{32,36}... | collective-permute-start | bytes 393224 | tf_op jit(solution)/shard_map/ppermute | solution.py:197
  26.7 0.0 copy-done.1
  26.8 0.0 copy-start
  26.8 1.2 %copy-done = bf16[128,4096]{1,0:T(8,128)(2,1)S(1)} copy-done((bf16[128,4096]{1,0:T(8,128)(2,1)S(1)}, bf16[128,4096]{1,0:T(8,128)(2,1)}, u32[]{:S(2)}) %copy-start) | copy-done | bytes 1048600
  28.0 1.9 %shard_map.68 = (f32[4,128,1024]{2,1,0:T(8,128)S(1)}, f32[2,16,256]{2,1,0:T(8,128)S(1)}, f32[128,128]{1,0:T(8,128)S(1)}, bf16[128,4096]{1,0:T(8,128)(2,1)S(1)}, bf16[128,512]{1,0:T(8,128)(2,1)S(1)}) custom-call(s32[1]{0:T(128)} %bitcast.base_ref, s32[32]{0:T(128)S(1)} %copy-done.1, bf16[128,4096]{1,0:T(8,128)(2,1)S(1)} %copy-done, bf16[128,512]{1,0:T(8,128)(2,1)} %k_ref.1, ...), custom_call_target="tpu_custom_call" | custom-call | flops 1342177280000 | bytes 4685956 | tf_op jit(solution)/shard_map/pallas_call | solution.py:172
  29.9 40.0 %collective-permute-done.k_far_ref = bf16[128,512]{1,0:T(8,128)(2,1)} collective-permute-done((bf16[128,512]{1,0:T(8,128)(2,1)}, bf16[128,512]{1,0:T(8,128)(2,1)}, u32[]{:S(2)}, u32[]{:S(2)}) %collective-permute-start) | collective-permute-done | bytes 131104 | tf_op jit(solution)/shard_map/ppermute | solution.py:196
  69.9 3.6 %collective-permute-done.1.v_far_ref = bf16[128,512]{1,0:T(8,128)(2,1)} collective-permute-done((bf16[128,512]{1,0:T(8,128)(2,1)}, bf16[128,512]{1,0:T(8,128)(2,1)}, u32[]{:S(2)}, u32[]{:S(2)}) %collective-permute-start.1) | collective-permute-done | bytes 131104 | tf_op jit(solution)/shard_map/ppermute | solution.py:197
  73.5 0.0 all-to-all-done.og_far_ref
  73.5 4.8 %shard_map.69 = (bf16[1024,128]{1,0:T(8,128)(2,1)S(1)}, bf16[4,128,1024]{2,1,0:T(8,128)(2,1)S(1)}, bf16[4,128,1024]{2,1,0:T(8,128)(2,1)S(1)}, f32[16,256]{1,0:T(8,128)S(1)}, bf16[16,128,256]{2,1,0:T(8,128)(2,1)S(1)}) custom-call(f32[4,128,1024]{2,1,0:T(8,128)S(1)} %get-tuple-element.12.e_ref, f32[2,16,256]{2,1,0:T(8,128)S(1)} %get-tuple-element.13.stats_ref, ...), custom_call_target="tpu_custom_call" | custom-call | flops 671088640 | bytes 8110080 | tf_op jit(solution)/shard_map/pallas_call | solution.py:172
  78.3 3.1 %collective-permute-start.2 = (bf16[1024,128]{1,0:T(8,128)(2,1)S(1)}, bf16[1024,128]{1,0:T(8,128)(2,1)S(1)}, u32[]{:S(2)}, u32[]{:S(2)}) collective-permute-start(bf16[1024,128]{1,0:T(8,128)(2,1)S(1)} %get-tuple-element.20), channel_id=1, source_target_pairs={{4,0},{8,4},{12,8},{16,12},{20,16},{24,20},{28,24},{32,28},{36,32}... | collective-permute-start | bytes 786440 | tf_op jit(solution)/shard_map/ppermute | solution.py:233
  81.3 0.8 shard_map.70.own_ref
  82.1 5.8 %collective-permute-done.2.halo_ref = bf16[1024,128]{1,0:T(8,128)(2,1)S(1)} collective-permute-done((bf16[1024,128]{1,0:T(8,128)(2,1)S(1)}, bf16[1024,128]{1,0:T(8,128)(2,1)S(1)}, u32[]{:S(2)}, u32[]{:S(2)}) %collective-permute-start.2) | collective-permute-done | bytes 262176 | tf_op jit(solution)/shard_map/ppermute | solution.py:233
  88.0 0.1 shard_map.71
  88.0 29.2 %all_to_all.10.got_ref = bf16[16,72,128]{2,1,0:T(8,128)(2,1)S(1)} all-to-all(bf16[16,72,128]{2,1,0:T(8,128)(2,1)S(1)} %shard_map.71), channel_id=1, replica_groups=mesh['span'=16,'head'=16,'rep'=4] {'head'}, dimensions={0} | all-to-all | bytes 589824 | tf_op jit(solution)/shard_map/all_to_all | solution.py:247
  117.2 0.8 shard_map.72
Async XLA Ops:
  0.6 26.1 %copy-start.1 = (s32[32]{0:T(128)S(1)}, s32[32]{0:T(128)}, u32[]{:S(2)}) copy-start(s32[32]{0:T(128)} %doc_ref.1) | copy-start | bytes 388
  0.6 72.8 %all-to-all-start = ((bf16[16,128,256]{2,1,0:T(8,128)(2,1)}), bf16[16,128,256]{2,1,0:T(8,128)(2,1)}, u32[]{:S(2)}, u32[]{:S(2)}) async-start(bf16[16,128,256]{2,1,0:T(8,128)(2,1)} %bitcast.2), calls=%async_computation | async-start | bytes 2097152 | tf_op jit(solution)/shard_map/all_to_all | solution.py:193
  19.6 50.3 %collective-permute-start = (bf16[128,512]{1,0:T(8,128)(2,1)}, bf16[128,512]{1,0:T(8,128)(2,1)}, u32[]{:S(2)}, u32[]{:S(2)}) collective-permute-start(bf16[128,512]{1,0:T(8,128)(2,1)} %k_ref.1), channel_id=1, source_target_pairs={{0,4},{4,8},{8,12},{12,16},{16,20},{20,24},{24,28},{28,32},{32,36}... | collective-permute-start | bytes 393224 | tf_op jit(solution)/shard_map/ppermute | solution.py:196
  23.4 50.1 %collective-permute-start.1 = (bf16[128,512]{1,0:T(8,128)(2,1)}, bf16[128,512]{1,0:T(8,128)(2,1)}, u32[]{:S(2)}, u32[]{:S(2)}) collective-permute-start(bf16[128,512]{1,0:T(8,128)(2,1)} %v_ref.1), channel_id=1, source_target_pairs={{0,4},{4,8},{8,12},{12,16},{16,20},{20,24},{24,28},{28,32},{32,36}... | collective-permute-start | bytes 393224 | tf_op jit(solution)/shard_map/ppermute | solution.py:197
  26.8 1.2 %copy-start = (bf16[128,4096]{1,0:T(8,128)(2,1)S(1)}, bf16[128,4096]{1,0:T(8,128)(2,1)}, u32[]{:S(2)}) copy-start(bf16[128,4096]{1,0:T(8,128)(2,1)} %q_ref.1) | copy-start | bytes 3145732
  78.3 9.7 %collective-permute-start.2 = (bf16[1024,128]{1,0:T(8,128)(2,1)S(1)}, bf16[1024,128]{1,0:T(8,128)(2,1)S(1)}, u32[]{:S(2)}, u32[]{:S(2)}) collective-permute-start(bf16[1024,128]{1,0:T(8,128)(2,1)S(1)} %get-tuple-element.20), channel_id=1, source_target_pairs={{4,0},{8,4},{12,8},{16,12},{20,16},{24,20},{28,24},{32,28},{36,32}... | collective-permute-start | bytes 786440 | tf_op jit(solution)/shard_map/ppermute | solution.py:233

commit v3 on v2

--- a/solution.py
+++ b/solution.py
@@ -55,11 +55,13 @@
     return slice(h * HEAD_DIM, (h + 1) * HEAD_DIM)
 
 
-def own_scores_kernel(
-    base_ref, doc_ref, q_ref, k_ref, v_ref, e_ref, stats_ref, bias_ref, q_out_ref, v_out_ref
+def forward_kernel(
+    base_ref, doc_ref, q_ref, k_ref, v_ref, prev_ref, p_ref, p_prev_ref, total_ref, q_out_ref, v_out_ref
 ):
+    features = KV_HEADS * HEAD_DIM
     q_out_ref[...] = q_ref[...]
-    v_out_ref[...] = v_ref[...]
+    v_out_ref[:BLOCK, :] = prev_ref[:, features:]
+    v_out_ref[BLOCK:, :] = v_ref[...]
     base = base_ref[0]
     query_pos = base + lax.broadcasted_iota(jnp.int32, (1, BLOCK), 1)
     doc_first = jnp.zeros((1, BLOCK), jnp.int32)
@@ -67,72 +69,54 @@
     for d in range(DOCS):
         doc_first = jnp.where(start <= query_pos, start, doc_first)
         start = start + doc_ref[d]
-    key_pos = base + lax.broadcasted_iota(jnp.int32, (BLOCK, BLOCK), 0)
-    bias_ref[...] = jnp.where(key_pos - BLOCK >= doc_first, 0.0, NEG)
+    key_pos = base - BLOCK + lax.broadcasted_iota(jnp.int32, (WIDTH, BLOCK), 0)
     bias = twice(jnp.where((key_pos >= doc_first) & (key_pos <= query_pos), 0.0, NEG))
     for g in range(KV_HEADS):
+        keys = jnp.concatenate([prev_ref[:, head_cols(g)], k_ref[:, head_cols(g)]], 0)
         for i in range(PAIRS):
             pair = g * PAIRS + i
-            s = dot(k_ref[:, head_cols(g)], pair_rows(q_ref, pair), NT) * SCORE_SCALE + bias
+            s = dot(keys, pair_rows(q_ref, pair), NT) * SCORE_SCALE + bias
             row_max = jnp.max(s, axis=0, keepdims=True)
             e = jnp.exp2(s - row_max)
-            e_ref[g, :, pair_cols(i)] = e
-            stats_ref[0, pair : pair + 1, :] = row_max
-            stats_ref[1, pair : pair + 1, :] = jnp.sum(e, axis=0, keepdims=True)
+            total = jnp.sum(e, axis=0, keepdims=True)
+            total_ref[pair : pair + 1, :] = (row_max + jnp.log2(total)) * math.log(2.0)
+            p = (e * (1.0 / total)).astype(jnp.bfloat16)
+            p_prev_ref[g, :, pair_cols(i)] = p[:BLOCK]
+            p_ref[g, :, pair_cols(i)] = p[BLOCK:]
 
 
 def halo_kernel(
-    e_ref, stats_ref, bias_ref, q_ref, v_ref, k_far_ref, v_far_ref, og_far_ref,
-    halo_ref, p_ref, ds_ref, total_ref, og_ref, p_prev_ref, ds_prev_ref, k_prev_ref, v_prev_ref, sems,
+    p_ref, p_prev_ref, q_ref, v_ref, og_far_ref, halo_ref, ds_ref, og_ref, ds_prev_ref, sems
 ):
-    copies = [
-        pltpu.make_async_copy(k_far_ref, k_prev_ref, sems.at[KV_HEADS]),
-        pltpu.make_async_copy(v_far_ref, v_prev_ref, sems.at[KV_HEADS + 1]),
-    ]
     og_copies = [
         pltpu.make_async_copy(
             og_far_ref.at[pl.ds(g * PAIRS, PAIRS)], og_ref.at[pl.ds(g * PAIRS, PAIRS)], sems.at[g]
         )
         for g in range(KV_HEADS)
     ]
-    for copy in copies + og_copies:
+    for copy in og_copies:
         copy.start()
-    for copy in copies:
+    for copy in og_copies:
         copy.wait()
-    bias = twice(bias_ref[...])
     for g in range(KV_HEADS):
-        og_copies[g].wait()
-        vals = jnp.concatenate([v_prev_ref[:, head_cols(g)], v_ref[:, head_cols(g)]], 0)
+        vals = v_ref[:, head_cols(g)]
         queries, grads = [], []
         for i in range(PAIRS):
             pair = g * PAIRS + i
-            q = pair_rows(q_ref, pair)
             og = pair_rows(og_ref.at[pair], 0)
-            queries.append(q)
+            queries.append(pair_rows(q_ref, pair))
             grads.append(og)
-            s = dot(k_prev_ref[:, head_cols(g)], q, NT) * SCORE_SCALE + bias
-            own_max = stats_ref[0, pair : pair + 1, :]
-            row_max = jnp.maximum(jnp.max(s, axis=0, keepdims=True), own_max)
-            e = jnp.exp2(s - row_max)
-            shrink = jnp.exp2(own_max - row_max)
-            total = jnp.sum(e, axis=0, keepdims=True) + shrink * stats_ref[1, pair : pair + 1, :]
-            total_ref[pair : pair + 1, :] = (row_max + jnp.log2(total)) * math.log(2.0)
-            inverse = 1.0 / total
-            p_prev = e * inverse
-            p_own = e_ref[g, :, pair_cols(i)] * (shrink * inverse)
+            p_prev = p_prev_ref[g, :, pair_cols(i)].astype(jnp.float32)
+            p_own = p_ref[g, :, pair_cols(i)].astype(jnp.float32)
             dp = dot(vals, og, NT)
             dp_prev, dp_own = dp[:BLOCK], dp[BLOCK:]
-            delta = jnp.sum(p_prev * dp_prev, axis=0, keepdims=True) + jnp.sum(
-                p_own * dp_own, axis=0, keepdims=True
-            )
-            p_prev_ref[:, pair_cols(i)] = p_prev.astype(jnp.bfloat16)
+            delta = jnp.sum(p_prev * dp_prev + p_own * dp_own, axis=0, keepdims=True)
             ds_prev_ref[:, pair_cols(i)] = (p_prev * (dp_prev - delta)).astype(jnp.bfloat16)
-            p_ref[g, :, pair_cols(i)] = p_own.astype(jnp.bfloat16)
             ds_ref[g, :, pair_cols(i)] = (p_own * (dp_own - delta)).astype(jnp.bfloat16)
         dk = dot(ds_prev_ref[...], jnp.concatenate(queries, 0)) * SCALE
-        dv = dot(p_prev_ref[...], jnp.concatenate(grads, 0))
-        halo_ref[feature_rows(g, 0), :] = dk.T.astype(jnp.bfloat16)
-        halo_ref[feature_rows(g, 1), :] = dv.T.astype(jnp.bfloat16)
+        dv = dot(p_prev_ref[g], jnp.concatenate(grads, 0))
+        halo_ref[feature_rows(g, 0), :] = dk.astype(jnp.bfloat16).T
+        halo_ref[feature_rows(g, 1), :] = dv.astype(jnp.bfloat16).T
 
 
 def own_kernel(p_ref, ds_ref, q_ref, og_ref, own_ref):
@@ -193,42 +177,35 @@
     og = lax.all_to_all(
         out_grad.reshape(owners, BLOCK, HEADS_OWNED * HEAD_DIM), "head", 0, 0, tiled=True
     )
-    k_prev = lax.ppermute(keys, ("span", "head"), onward)
-    v_prev = lax.ppermute(values, ("span", "head"), onward)
+    prev = lax.ppermute(jnp.concatenate([keys, values], 1), ("span", "head"), onward)
     macs = HEADS * BLOCK * BLOCK * HEAD_DIM
     array = jax.ShapeDtypeStruct
-    exponents, stats, bias, held_queries, held_values = call(
-        own_scores_kernel,
+    kept = array((KV_HEADS, BLOCK, GROUP * BLOCK), bf16)
+    weights, halo_weights, totals, held_queries, held_values = call(
+        forward_kernel,
         (
-            array((KV_HEADS, BLOCK, GROUP * BLOCK), f32),
-            array((2, owners, HEADS_OWNED * BLOCK), f32),
-            array((BLOCK, BLOCK), f32),
-            array(queries.shape, bf16),
-            array(values.shape, bf16),
-        ),
-        (base, doc_lengths, queries, keys, values),
-        [SMEM, SMEM] + [VMEM] * 3,
-        flops=20000 * macs,
-        exps=HEADS * BLOCK * BLOCK,
-    )
-    features = 2 * KV_HEADS * HEAD_DIM
-    kept = array((KV_HEADS, BLOCK, GROUP * BLOCK), bf16)
-    halo, weights, dscores, totals, held_grads = call(
-        halo_kernel,
-        (
-            array((features, BLOCK), bf16),
             kept,
             kept,
             array((owners, HEADS_OWNED * BLOCK), f32),
-            array(og.shape, bf16),
-        ),
-        (exponents, stats, bias, held_queries, held_values, k_prev, v_prev, og),
-        [VMEM] * 5 + [pl.BlockSpec(memory_space=pl.ANY)] * 3,
-        scratch=[pltpu.VMEM((BLOCK, GROUP * BLOCK), bf16)] * 2
-        + [pltpu.VMEM(values.shape, bf16)] * 2
-        + [pltpu.SemaphoreType.DMA((KV_HEADS + 2,))],
-        flops=10 * macs,
-        exps=HEADS * BLOCK * BLOCK,
+            array(queries.shape, bf16),
+            array((WIDTH, KV_HEADS * HEAD_DIM), bf16),
+        ),
+        (base, doc_lengths, queries, keys, values, prev),
+        [SMEM, SMEM] + [VMEM] * 4,
+        flops=20000 * macs,
+        exps=HEADS * BLOCK * WIDTH,
+    )
+    features = 2 * KV_HEADS * HEAD_DIM
+    halo, dscores, held_grads = call(
+        halo_kernel,
+        (array((features, BLOCK), bf16), kept, array(og.shape, bf16)),
+        (weights, halo_weights, held_queries, held_values, og),
+        [VMEM] * 4 + [pl.BlockSpec(memory_space=pl.ANY)],
+        scratch=[
+            pltpu.VMEM((BLOCK, GROUP * BLOCK), bf16),
+            pltpu.SemaphoreType.DMA((KV_HEADS,)),
+        ],
+        flops=8 * macs,
     )
     returned = lax.ppermute(halo, ("span", "head"), back)
     own = call(

time: 118 us -> 117 us (level)
  starting transfers between devices: 29.1 us -> 24.4 us
  local copies, waits for them, and re-layouts: 1.22 us -> 3.79 us
    ppermute x2 -> x1, waiting for transfers between devices: 43.6 us -> 1.99 us  [shards(): lax.ppermute(jnp.concatenate([keys, values], 1), ('span', 'head'), onward)]
    all_to_all x1, waiting for transfers between devices: 0.01 us -> 41.4 us  [shards(): lax.all_to_all(out_grad.reshape(owners, BLOCK, HEADS_OWNED * HEAD_DIM), '...]
    ppermute x2 -> x1, starting transfers between devices: 7.15 us -> 4.28 us  [shards(): lax.ppermute(jnp.concatenate([keys, values], 1), ('span', 'head'), onward)]
    unnamed x4 -> x12, local copies, waits for them, and re-layouts: 1.22 us -> 3.79 us
  transfers between devices with their start and end apart: 4 -> 3, of which waited for: 3 -> 3; matrix products, arithmetic and copies ran while one was open for 0% -> 0% of each run, Pallas kernels for 2% -> 3%
where the time goes in v3:
time: 117 us
  waiting for transfers between devices  48.9 us (42%)
  blocking collectives  30.1 us (26%)
  starting transfers between devices  24.4 us (21%)
  Pallas kernels  7.62 us (7%)
  local copies, waits for them, and re-layouts  3.79 us (3%)
    all_to_all x1, waiting for transfers between devices, shards(): lax.all_to_all(out_grad.reshape(owners, BLOCK, HEADS_OWNED * HEAD_DIM), '...  41.4 us
    all_to_all x1, blocking collectives, shards(): got = lax.all_to_all(send, 'head', 0, 0, tiled=True)  30.1 us
    all_to_all x1, starting transfers between devices, shards(): lax.all_to_all(out_grad.reshape(owners, BLOCK, HEADS_OWNED * HEAD_DIM), '...  18.2 us
    pallas_call x5, Pallas kernels, call(): pl.pallas_call(kernel, out_shape=out_shape, in_specs=specs, out_specs=jax...  7.62 us
    ppermute x1, waiting for transfers between devices, shards(): returned = lax.ppermute(halo, ('span', 'head'), back)  5.57 us
    ppermute x1, starting transfers between devices, shards(): lax.ppermute(jnp.concatenate([keys, values], 1), ('span', 'head'), onward)  4.28 us
    unnamed x12, local copies, waits for them, and re-layouts  3.79 us
  transfers between devices with their start and end apart: 3, of which 3 were waited for; matrix products, arithmetic and copies ran while one was open for 0% of the time, Pallas kernels for 3%

profile of v3, /device:TPU:56, one launch (start us, length us, event | category | flops | bytes accessed | tf_op | source)
XLA Modules:
  0.0 116.5 jit_solution(17341479345206547574)
XLA Ops:
  0.6 1.0 pad_maximum_fusion
  1.6 4.3 %collective-permute-start = (bf16[128,1024]{1,0:T(8,128)(2,1)S(1)}, bf16[128,1024]{1,0:T(8,128)(2,1)S(1)}, u32[]{:S(2)}, u32[]{:S(2)}) collective-permute-start(bf16[128,1024]{1,0:T(8,128)(2,1)S(1)} %pad_maximum_fusion), channel_id=1, source_target_pairs={{0,4},{4,8},{8,12},{12,16},{16,20},{20,24},{24,28},{28,32},{32,36}... | collective-permute-start | bytes 786440 | tf_op jit(solution)/shard_map/ppermute | solution.py:180
  5.9 0.0 copy-start
  5.9 18.2 %all-to-all-start = ((bf16[16,128,256]{2,1,0:T(8,128)(2,1)}), bf16[16,128,256]{2,1,0:T(8,128)(2,1)}, u32[]{:S(2)}, u32[]{:S(2)}) async-start(bf16[16,128,256]{2,1,0:T(8,128)(2,1)} %bitcast.2), calls=%async_computation | async-start | bytes 2097152 | tf_op jit(solution)/shard_map/all_to_all | solution.py:177
  24.1 0.0 copy-start.5
  24.1 2.0 %collective-permute-done.prev_ref = bf16[128,1024]{1,0:T(8,128)(2,1)S(1)} collective-permute-done((bf16[128,1024]{1,0:T(8,128)(2,1)S(1)}, bf16[128,1024]{1,0:T(8,128)(2,1)S(1)}, u32[]{:S(2)}, u32[]{:S(2)}) %collective-permute-start) | collective-permute-done | bytes 262176 | tf_op jit(solution)/shard_map/ppermute | solution.py:180
  26.1 0.0 copy-start.3
  26.1 0.7 copy-done.3
  26.8 0.0 copy-done
  26.8 0.0 copy-done.5
  26.8 0.0 copy-start.1
  26.8 0.9 copy-done.1
  27.7 0.0 copy-start.2
  27.7 1.2 %copy-done.2 = bf16[128,4096]{1,0:T(8,128)(2,1)S(1)} copy-done((bf16[128,4096]{1,0:T(8,128)(2,1)S(1)}, bf16[128,4096]{1,0:T(8,128)(2,1)}, u32[]{:S(2)}) %copy-start.2) | copy-done | bytes 1048600
  28.9 0.9 copy-done.4
  29.9 2.5 %shard_map.68 = (bf16[4,128,1024]{2,1,0:T(8,128)(2,1)S(1)}, bf16[4,128,1024]{2,1,0:T(8,128)(2,1)S(1)}, f32[16,256]{1,0:T(8,128)S(1)}, bf16[128,4096]{1,0:T(8,128)(2,1)S(1)}, bf16[256,512]{1,0:T(8,128)(2,1)S(1)}) custom-call(s32[1]{0:T(128)} %bitcast.base_ref, s32[32]{0:T(128)S(1)} %copy-done.5, bf16[128,4096]{1,0:T(8,128)(2,1)S(1)} %copy-done.2, ...), custom_call_target="tpu_custom_call" | custom-call | flops 1342177280000 | bytes 4997252 | tf_op jit(solution)/shard_map/pallas_call | solution.py:156
  32.4 41.4 %all-to-all-done.og_far_ref = bf16[16,128,256]{2,1,0:T(8,128)(2,1)} async-done(((bf16[16,128,256]{2,1,0:T(8,128)(2,1)}), bf16[16,128,256]{2,1,0:T(8,128)(2,1)}, u32[]{:S(2)}, u32[]{:S(2)}) %all-to-all-start) | async-done | bytes 1048608 | tf_op jit(solution)/shard_map/all_to_all | solution.py:177
  73.8 3.5 %shard_map.69 = (bf16[1024,128]{1,0:T(8,128)(2,1)S(1)}, bf16[4,128,1024]{2,1,0:T(8,128)(2,1)S(1)}, bf16[16,128,256]{2,1,0:T(8,128)(2,1)S(1)}) custom-call(bf16[4,128,1024]{2,1,0:T(8,128)(2,1)S(1)} %get-tuple-element.10.p_ref, bf16[4,128,1024]{2,1,0:T(8,128)(2,1)S(1)} %get-tuple-element.11.p_prev_ref, bf16[128,4096]{1,0:T(8,128)(2,1)S(1)} %get-tuple-element.12.q_ref, ...), custom_call_target="tpu_custom_call" | custom-call | flops 536870912 | bytes 6815744 | tf_op jit(solution)/shard_map/pallas_call | solution.py:156
  77.3 1.9 %collective-permute-start.1 = (bf16[1024,128]{1,0:T(8,128)(2,1)S(1)}, bf16[1024,128]{1,0:T(8,128)(2,1)S(1)}, u32[]{:S(2)}, u32[]{:S(2)}) collective-permute-start(bf16[1024,128]{1,0:T(8,128)(2,1)S(1)} %get-tuple-element.16), channel_id=1, source_target_pairs={{4,0},{8,4},{12,8},{16,12},{20,16},{24,20},{28,24},{32,28},{36,32}... | collective-permute-start | bytes 786440 | tf_op jit(solution)/shard_map/ppermute | solution.py:210
  79.2 0.8 shard_map.70.own_ref
  80.0 5.6 %collective-permute-done.1.halo_ref = bf16[1024,128]{1,0:T(8,128)(2,1)S(1)} collective-permute-done((bf16[1024,128]{1,0:T(8,128)(2,1)S(1)}, bf16[1024,128]{1,0:T(8,128)(2,1)S(1)}, u32[]{:S(2)}, u32[]{:S(2)}) %collective-permute-start.1) | collective-permute-done | bytes 262176 | tf_op jit(solution)/shard_map/ppermute | solution.py:210
  85.6 0.1 shard_map.71
  85.6 30.1 %all_to_all.10.got_ref = bf16[16,72,128]{2,1,0:T(8,128)(2,1)S(1)} all-to-all(bf16[16,72,128]{2,1,0:T(8,128)(2,1)S(1)} %shard_map.71), channel_id=1, replica_groups=mesh['span'=16,'head'=16,'rep'=4] {'head'}, dimensions={0} | all-to-all | bytes 589824 | tf_op jit(solution)/shard_map/all_to_all | solution.py:224
  115.8 0.8 shard_map.72
  (1 shorter events, 0.0 us)
Async XLA Ops:
  1.6 24.5 %collective-permute-start = (bf16[128,1024]{1,0:T(8,128)(2,1)S(1)}, bf16[128,1024]{1,0:T(8,128)(2,1)S(1)}, u32[]{:S(2)}, u32[]{:S(2)}) collective-permute-start(bf16[128,1024]{1,0:T(8,128)(2,1)S(1)} %pad_maximum_fusion), channel_id=1, source_target_pairs={{0,4},{4,8},{8,12},{12,16},{16,20},{20,24},{24,28},{28,32},{32,36}... | collective-permute-start | bytes 786440 | tf_op jit(solution)/shard_map/ppermute | solution.py:180
  5.9 20.9 %copy-start = (bf16[128,512]{1,0:T(8,128)(2,1)S(1)}, bf16[128,512]{1,0:T(8,128)(2,1)}, u32[]{:S(2)}) copy-start(bf16[128,512]{1,0:T(8,128)(2,1)} %k_ref.1) | copy-start | bytes 393220
  5.9 67.9 %all-to-all-start = ((bf16[16,128,256]{2,1,0:T(8,128)(2,1)}), bf16[16,128,256]{2,1,0:T(8,128)(2,1)}, u32[]{:S(2)}, u32[]{:S(2)}) async-start(bf16[16,128,256]{2,1,0:T(8,128)(2,1)} %bitcast.2), calls=%async_computation | async-start | bytes 2097152 | tf_op jit(solution)/shard_map/all_to_all | solution.py:177
  24.1 2.7 %copy-start.5 = (s32[32]{0:T(128)S(1)}, s32[32]{0:T(128)}, u32[]{:S(2)}) copy-start(s32[32]{0:T(128)} %doc_ref.1) | copy-start | bytes 388
  26.1 0.7 copy-start.3
  26.8 0.9 copy-start.1
  27.7 1.2 %copy-start.2 = (bf16[128,4096]{1,0:T(8,128)(2,1)S(1)}, bf16[128,4096]{1,0:T(8,128)(2,1)}, u32[]{:S(2)}) copy-start(bf16[128,4096]{1,0:T(8,128)(2,1)} %q_ref.1) | copy-start | bytes 3145732
  28.9 0.9 copy-start.4
  77.3 8.3 %collective-permute-start.1 = (bf16[1024,128]{1,0:T(8,128)(2,1)S(1)}, bf16[1024,128]{1,0:T(8,128)(2,1)S(1)}, u32[]{:S(2)}, u32[]{:S(2)}) collective-permute-start(bf16[1024,128]{1,0:T(8,128)(2,1)S(1)} %get-tuple-element.16), channel_id=1, source_target_pairs={{4,0},{8,4},{12,8},{16,12},{20,16},{24,20},{28,24},{32,28},{36,32}... | collective-permute-start | bytes 786440 | tf_op jit(solution)/shard_map/ppermute | solution.py:210

commit v4 on v3

v4 whole, which is shorter than its diff:
```python
import math

import jax
import jax.numpy as jnp
from jax import lax
from jax.experimental import pallas as pl
from jax.experimental.pallas import tpu as pltpu
from jax.sharding import PartitionSpec as P

HEADS = 32
KV_HEADS = 4
GROUP = HEADS // KV_HEADS
HEAD_DIM = 128
BLOCK = 128
WIDTH = 2 * BLOCK
DOCS = 32
OWNERS = 16
OWNED = 2 * KV_HEADS * HEAD_DIM // OWNERS
HEADS_OWNED = HEADS // OWNERS
EXTRA = 8
SCALE = 1.0 / math.sqrt(HEAD_DIM)
SCORE_SCALE = SCALE * math.log2(math.e)
NEG = -1e30
PAIRS = GROUP // 2
VMEM = pl.BlockSpec(memory_space=pltpu.VMEM)
SMEM = pl.BlockSpec(memory_space=pltpu.SMEM)
NT = (((1,), (1,)), ((), ()))


def dot(a, b, dims=(((1,), (0,)), ((), ()))):
    return lax.dot_general(a, b, dims, preferred_element_type=jnp.float32)


def feature_rows(group, which):
    first = (2 * group + which) * HEAD_DIM
    return slice(first, first + HEAD_DIM)


def head_cols(h):
    return slice(h * HEAD_DIM, (h + 1) * HEAD_DIM)


def forward_kernel(
    base_ref, doc_ref, q_ref, k_ref, v_ref, prev_ref, p_ref, total_ref, qt_ref, v_out_ref
):
    features = KV_HEADS * HEAD_DIM
    v_out_ref[:BLOCK, :] = prev_ref[:, features:]
    v_out_ref[BLOCK:, :] = v_ref[...]
    base = base_ref[0]
    query_pos = base + lax.broadcasted_iota(jnp.int32, (BLOCK, 1), 0)
    doc_first = jnp.zeros((BLOCK, 1), jnp.int32)
    start = jnp.int32(0)
    for d in range(DOCS):
        doc_first = jnp.where(start <= query_pos, start, doc_first)
        start = start + doc_ref[d]
    key_pos = base - BLOCK + lax.broadcasted_iota(jnp.int32, (BLOCK, WIDTH), 1)
    bias = jnp.where((key_pos >= doc_first) & (key_pos <= query_pos), 0.0, NEG)
    for g in range(KV_HEADS):
        keys = jnp.concatenate([prev_ref[:, head_cols(g)], k_ref[:, head_cols(g)]], 0)
        for h in range(GROUP):
            head = g * GROUP + h
            q = q_ref[:, head_cols(head)]
            qt_ref[g, :, head_cols(h)] = q.T
            s = dot(q, keys, NT) * SCORE_SCALE + bias
            row_max = jnp.max(s, axis=1, keepdims=True)
            e = jnp.exp2(s - row_max)
            total = jnp.sum(e, axis=1, keepdims=True)
            log_total = (row_max + jnp.log2(total)) * math.log(2.0)
            total_ref[head : head + 1, :] = jnp.broadcast_to(log_total, (BLOCK, BLOCK)).T[:1]
            p_ref[g, head_cols(h), :] = (e * (1.0 / total)).astype(jnp.bfloat16)


def backward_kernel(p_ref, qt_ref, v_ref, og_far_ref, halo_ref, own_ref, og_ref, sems):
    copies = [
        pltpu.make_async_copy(
            og_far_ref.at[pl.ds(g * PAIRS, PAIRS)], og_ref.at[pl.ds(g * PAIRS, PAIRS)], sems.at[g]
        )
        for g in range(KV_HEADS)
    ]
    for copy in copies:
        copy.start()
    for copy in copies:
        copy.wait()
    for g in range(KV_HEADS):
        vals = v_ref[:, head_cols(g)]
        dss, ogs = [], []
        for h in range(GROUP):
            og = og_ref[g * PAIRS + h // 2, :, head_cols(h % 2)]
            dp = dot(og, vals, NT)
            p = p_ref[g, h * BLOCK : (h + 1) * BLOCK, :].astype(jnp.float32)
            delta = jnp.sum(p * dp, axis=1, keepdims=True)
            dss.append((p * (dp - delta)).astype(jnp.bfloat16))
            ogs.append(og.T)
        dk = dot(qt_ref[g], jnp.concatenate(dss, 0)) * SCALE
        dv = dot(jnp.concatenate(ogs, 1), p_ref[g])
        for i, grad in enumerate((dk, dv)):
            halo_ref[feature_rows(g, i), :] = grad[:, :BLOCK].astype(jnp.bfloat16)
            own_ref[feature_rows(g, i), :] = grad[:, BLOCK:]


def sum_kernel(own_ref, halo_ref, total_ref, send_ref):
    for z in range(OWNERS):
        rows = slice(z * OWNED, (z + 1) * OWNED)
        send_ref[z, :OWNED, :] = (
            own_ref[rows, :] + halo_ref[rows, :].astype(jnp.float32)
        ).astype(jnp.bfloat16)
        total = total_ref[z * HEADS_OWNED : (z + 1) * HEADS_OWNED, :]
        high = total.astype(jnp.bfloat16).astype(jnp.float32)
        low = total - high
        pad = jnp.zeros((EXTRA - 2 * HEADS_OWNED, BLOCK), jnp.float32)
        send_ref[z, OWNED:, :] = jnp.concatenate([high, low, pad], 0).astype(jnp.bfloat16)


def unpack_kernel(got_ref, grads_ref, total_ref):
    for b in range(OWNERS):
        cols = slice(b * BLOCK, (b + 1) * BLOCK)
        grads_ref[:, cols] = got_ref[b, :OWNED, :]
        extra = got_ref[b, OWNED:, :].astype(jnp.float32)
        total_ref[:, cols] = extra[:HEADS_OWNED] + extra[HEADS_OWNED : 2 * HEADS_OWNED]


def call(kernel, out_shape, args, specs, scratch=(), flops=0, exps=0, limit=8):
    outs = jax.tree.leaves(out_shape)
    moved = sum(math.prod(a.shape) * a.dtype.itemsize for a in [*args, *outs])
    return pl.pallas_call(
        kernel,
        out_shape=out_shape,
        in_specs=specs,
        out_specs=jax.tree.map(lambda _: VMEM, out_shape),
        scratch_shapes=scratch,
        compiler_params=pltpu.CompilerParams(vmem_limit_bytes=limit * 2**20),
        cost_estimate=pl.CostEstimate(
            flops=flops, bytes_accessed=moved, transcendentals=exps
        ),
    )(*args)


def shards(queries, keys, values, out_grad, doc_lengths):
    spans, owners = lax.axis_size("span"), lax.axis_size("head")
    block_index = lax.axis_index("span") * owners + lax.axis_index("head")
    blocks = spans * owners
    base = jnp.full((1,), block_index * BLOCK, jnp.int32)
    f32, bf16 = jnp.float32, jnp.bfloat16
    onward = [(i, i + 1) for i in range(blocks - 1)]
    back = [(i + 1, i) for i in range(blocks - 1)]
    og = lax.all_to_all(
        out_grad.reshape(owners, BLOCK, HEADS_OWNED * HEAD_DIM), "head", 0, 0, tiled=True
    )
    prev = lax.ppermute(jnp.concatenate([keys, values], 1), ("span", "head"), onward)
    macs = HEADS * BLOCK * BLOCK * HEAD_DIM
    array = jax.ShapeDtypeStruct
    weights, totals, turned_queries, held_values = call(
        forward_kernel,
        (
            array((KV_HEADS, GROUP * BLOCK, WIDTH), bf16),
            array((HEADS, BLOCK), f32),
            array((KV_HEADS, HEAD_DIM, GROUP * BLOCK), bf16),
            array((WIDTH, KV_HEADS * HEAD_DIM), bf16),
        ),
        (base, doc_lengths, queries, keys, values, prev),
        [SMEM, SMEM] + [VMEM] * 4,
        flops=20000 * macs,
        exps=HEADS * BLOCK * WIDTH,
    )
    features = 2 * KV_HEADS * HEAD_DIM
    halo, own = call(
        backward_kernel,
        (array((features, BLOCK), bf16), array((features, BLOCK), f32)),
        (weights, turned_queries, held_values, og),
        [VMEM] * 3 + [pl.BlockSpec(memory_space=pl.ANY)],
        scratch=[
            pltpu.VMEM((owners, BLOCK, HEADS_OWNED * HEAD_DIM), bf16),
            pltpu.SemaphoreType.DMA((KV_HEADS,)),
        ],
        flops=12 * macs,
    )
    returned = lax.ppermute(halo, ("span", "head"), back)
    send = call(
        sum_kernel,
        array((owners, OWNED + EXTRA, BLOCK), bf16),
        (own, returned, totals),
        [VMEM] * 3,
    )
    got = lax.all_to_all(send, "head", 0, 0, tiled=True)
    return call(
        unpack_kernel,
        (
            array((OWNED, owners * BLOCK), bf16),
            array((HEADS_OWNED, owners * BLOCK), f32),
        ),
        (got,),
        [VMEM],
    )


def solution(mesh):
    return jax.shard_map(
        shards,
        mesh=mesh,
        in_specs=(
            P(("rep", "span", "head"), None),
            P(("rep", "span", "head"), None),
            P(("rep", "span", "head"), None),
            P(("rep", "span"), "head"),
            P("rep"),
        ),
        out_specs=(P("head", ("rep", "span")), P("head", ("rep", "span"))),
        check_vma=False,
    )
```

time: 117 us -> 117 us (level)
  waiting for transfers between devices: 48.9 us -> 46.5 us
  Pallas kernels: 7.62 us -> 9.18 us
    all_to_all x1, waiting for transfers between devices: 41.4 us -> 38 us  [shards(): lax.all_to_all(out_grad.reshape(owners, BLOCK, HEADS_OWNED * HEAD_DIM), '...]
    pallas_call x5 -> x4, Pallas kernels: 7.62 us -> 9.18 us  [call(): pl.pallas_call(kernel, out_shape=out_shape, in_specs=specs, out_specs=jax...]
  transfers between devices with their start and end apart: 3 -> 3, of which waited for: 3 -> 3; matrix products, arithmetic and copies ran while one was open for 0% -> 0% of each run, Pallas kernels for 3% -> 4%
where the time goes in v4:
time: 117 us; the launch traced here: 116 us
  waiting for transfers between devices  46.5 us (40%)
  blocking collectives  30.1 us (26%)
  starting transfers between devices  24.2 us (21%)
  Pallas kernels  9.18 us (8%)
  local copies, waits for them, and re-layouts  4.44 us (4%)
    all_to_all x1, waiting for transfers between devices, shards(): lax.all_to_all(out_grad.reshape(owners, BLOCK, HEADS_OWNED * HEAD_DIM), '...  38 us
    all_to_all x1, blocking collectives, shards(): got = lax.all_to_all(send, 'head', 0, 0, tiled=True)  30.1 us
    all_to_all x1, starting transfers between devices, shards(): lax.all_to_all(out_grad.reshape(owners, BLOCK, HEADS_OWNED * HEAD_DIM), '...  18 us
    pallas_call x4, Pallas kernels, call(): pl.pallas_call(kernel, out_shape=out_shape, in_specs=specs, out_specs=jax...  9.18 us
    ppermute x1, waiting for transfers between devices, shards(): returned = lax.ppermute(halo, ('span', 'head'), back)  6.34 us
    unnamed x12, local copies, waits for them, and re-layouts  4.44 us
    ppermute x1, starting transfers between devices, shards(): lax.ppermute(jnp.concatenate([keys, values], 1), ('span', 'head'), onward)  4.28 us
  transfers between devices with their start and end apart: 3, of which 3 were waited for; matrix products, arithmetic and copies ran while one was open for 0% of the time, Pallas kernels for 4%

profile of v4, /device:TPU:56, one launch (start us, length us, event | category | flops | bytes accessed | tf_op | source)
XLA Modules:
  0.0 116.2 jit_solution(6985125799992227303)
XLA Ops:
  0.6 0.0 copy-start
  0.6 1.0 pad_maximum_fusion
  1.7 4.3 %collective-permute-start = (bf16[128,1024]{1,0:T(8,128)(2,1)S(1)}, bf16[128,1024]{1,0:T(8,128)(2,1)S(1)}, u32[]{:S(2)}, u32[]{:S(2)}) collective-permute-start(bf16[128,1024]{1,0:T(8,128)(2,1)S(1)} %pad_maximum_fusion), channel_id=1, source_target_pairs={{0,4},{4,8},{8,12},{12,16},{16,20},{20,24},{24,28},{28,32},{32,36}... | collective-permute-start | bytes 786440 | tf_op jit(solution)/shard_map/ppermute | solution.py:149
  6.0 18.0 %all-to-all-start = ((bf16[16,128,256]{2,1,0:T(8,128)(2,1)}), bf16[16,128,256]{2,1,0:T(8,128)(2,1)}, u32[]{:S(2)}, u32[]{:S(2)}) async-start(bf16[16,128,256]{2,1,0:T(8,128)(2,1)} %bitcast.2), calls=%async_computation | async-start | bytes 2097152 | tf_op jit(solution)/shard_map/all_to_all | solution.py:146
  24.0 2.1 %collective-permute-done.prev_ref = bf16[128,1024]{1,0:T(8,128)(2,1)S(1)} collective-permute-done((bf16[128,1024]{1,0:T(8,128)(2,1)S(1)}, bf16[128,1024]{1,0:T(8,128)(2,1)S(1)}, u32[]{:S(2)}, u32[]{:S(2)}) %collective-permute-start) | collective-permute-done | bytes 262176 | tf_op jit(solution)/shard_map/ppermute | solution.py:149
  26.1 0.0 copy-start.3
  26.1 0.7 copy-done.3
  26.8 0.0 copy-done
  26.8 0.0 copy-start.1
  26.9 0.9 copy-done.1
  27.8 0.0 copy-start.2
  27.8 1.2 %copy-done.2 = bf16[128,4096]{1,0:T(8,128)(2,1)S(1)} copy-done((bf16[128,4096]{1,0:T(8,128)(2,1)S(1)}, bf16[128,4096]{1,0:T(8,128)(2,1)}, u32[]{:S(2)}) %copy-start.2) | copy-done | bytes 1048600
  29.0 0.0 copy-start.4
  29.0 0.9 copy-done.4
  29.9 0.0 copy-start.5
  29.9 0.7 copy-done.5
  30.6 5.1 %shard_map.68 = (bf16[4,1024,256]{2,1,0:T(8,128)(2,1)S(1)}, f32[32,128]{1,0:T(8,128)S(1)}, bf16[4,128,1024]{2,1,0:T(8,128)(2,1)S(1)}, bf16[256,512]{1,0:T(8,128)(2,1)S(1)}) custom-call(s32[1]{0:T(128)} %bitcast.base_ref, s32[32]{0:T(128)S(1)} %copy-done.5, bf16[128,4096]{1,0:T(8,128)(2,1)S(1)} %copy-done.2, bf16[128,512]{1,0:T(8,128)(2,1)S(1)} %copy-done, ...), custom_call_target="tpu_custom_call" | custom-call | flops 1342177280000 | bytes 4997252 | tf_op jit(solution)/shard_map/pallas_call | solution.py:125
  35.7 38.0 %all-to-all-done.og_far_ref = bf16[16,128,256]{2,1,0:T(8,128)(2,1)} async-done(((bf16[16,128,256]{2,1,0:T(8,128)(2,1)}), bf16[16,128,256]{2,1,0:T(8,128)(2,1)}, u32[]{:S(2)}, u32[]{:S(2)}) %all-to-all-start) | async-done | bytes 1048608 | tf_op jit(solution)/shard_map/all_to_all | solution.py:146
  73.7 3.2 %shard_map.69 = (bf16[1024,128]{1,0:T(8,128)(2,1)S(1)}, f32[1024,128]{1,0:T(8,128)S(1)}) custom-call(bf16[4,1024,256]{2,1,0:T(8,128)(2,1)S(1)} %get-tuple-element.8.p_ref, bf16[4,128,1024]{2,1,0:T(8,128)(2,1)S(1)} %get-tuple-element.9.qt_ref, bf16[256,512]{1,0:T(8,128)(2,1)S(1)} %get-tuple-element.10.v_ref, bf16[16,128,256]{2,1,0:T(8,128)(2,1)} %all-to-all-done.og_far_ref), custom_call_target="tpu_custom_call" | custom-call | flops 805306368 | bytes 5242880 | tf_op jit(solution)/shard_map/pallas_call | solution.py:125
  76.9 1.9 %collective-permute-start.1 = (bf16[1024,128]{1,0:T(8,128)(2,1)S(1)}, bf16[1024,128]{1,0:T(8,128)(2,1)S(1)}, u32[]{:S(2)}, u32[]{:S(2)}) collective-permute-start(bf16[1024,128]{1,0:T(8,128)(2,1)S(1)} %get-tuple-element.12), channel_id=1, source_target_pairs={{4,0},{8,4},{12,8},{16,12},{20,16},{24,20},{28,24},{32,28},{36,32}... | collective-permute-start | bytes 786440 | tf_op jit(solution)/shard_map/ppermute | solution.py:177
  78.9 6.3 %collective-permute-done.1.halo_ref = bf16[1024,128]{1,0:T(8,128)(2,1)S(1)} collective-permute-done((bf16[1024,128]{1,0:T(8,128)(2,1)S(1)}, bf16[1024,128]{1,0:T(8,128)(2,1)S(1)}, u32[]{:S(2)}, u32[]{:S(2)}) %collective-permute-start.1) | collective-permute-done | bytes 262176 | tf_op jit(solution)/shard_map/ppermute | solution.py:177
  85.2 0.1 shard_map.70
  85.3 30.1 %all_to_all.10.got_ref = bf16[16,72,128]{2,1,0:T(8,128)(2,1)S(1)} all-to-all(bf16[16,72,128]{2,1,0:T(8,128)(2,1)S(1)} %shard_map.70), channel_id=1, replica_groups=mesh['span'=16,'head'=16,'rep'=4] {'head'}, dimensions={0} | all-to-all | bytes 589824 | tf_op jit(solution)/shard_map/all_to_all | solution.py:184
  115.4 0.8 shard_map.71
Async XLA Ops:
  0.6 26.2 %copy-start = (bf16[128,512]{1,0:T(8,128)(2,1)S(1)}, bf16[128,512]{1,0:T(8,128)(2,1)}, u32[]{:S(2)}) copy-start(bf16[128,512]{1,0:T(8,128)(2,1)} %k_ref.1) | copy-start | bytes 393220
  1.7 24.5 %collective-permute-start = (bf16[128,1024]{1,0:T(8,128)(2,1)S(1)}, bf16[128,1024]{1,0:T(8,128)(2,1)S(1)}, u32[]{:S(2)}, u32[]{:S(2)}) collective-permute-start(bf16[128,1024]{1,0:T(8,128)(2,1)S(1)} %pad_maximum_fusion), channel_id=1, source_target_pairs={{0,4},{4,8},{8,12},{12,16},{16,20},{20,24},{24,28},{28,32},{32,36}... | collective-permute-start | bytes 786440 | tf_op jit(solution)/shard_map/ppermute | solution.py:149
  6.0 67.7 %all-to-all-start = ((bf16[16,128,256]{2,1,0:T(8,128)(2,1)}), bf16[16,128,256]{2,1,0:T(8,128)(2,1)}, u32[]{:S(2)}, u32[]{:S(2)}) async-start(bf16[16,128,256]{2,1,0:T(8,128)(2,1)} %bitcast.2), calls=%async_computation | async-start | bytes 2097152 | tf_op jit(solution)/shard_map/all_to_all | solution.py:146
  26.1 0.7 copy-start.3
  26.8 0.9 copy-start.1
  27.8 1.2 %copy-start.2 = (bf16[128,4096]{1,0:T(8,128)(2,1)S(1)}, bf16[128,4096]{1,0:T(8,128)(2,1)}, u32[]{:S(2)}) copy-start(bf16[128,4096]{1,0:T(8,128)(2,1)} %q_ref.1) | copy-start | bytes 3145732
  29.0 0.9 copy-start.4
  29.9 0.7 copy-start.5
  76.9 8.3 %collective-permute-start.1 = (bf16[1024,128]{1,0:T(8,128)(2,1)S(1)}, bf16[1024,128]{1,0:T(8,128)(2,1)S(1)}, u32[]{:S(2)}, u32[]{:S(2)}) collective-permute-start(bf16[1024,128]{1,0:T(8,128)(2,1)S(1)} %get-tuple-element.12), channel_id=1, source_target_pairs={{4,0},{8,4},{12,8},{16,12},{20,16},{24,20},{28,24},{32,28},{36,32}... | collective-permute-start | bytes 786440 | tf_op jit(solution)/shard_map/ppermute | solution.py:177

commit v5 on v4

--- a/solution.py
+++ b/solution.py
@@ -41,11 +41,8 @@
 
 
 def forward_kernel(
-    base_ref, doc_ref, q_ref, k_ref, v_ref, prev_ref, p_ref, total_ref, qt_ref, v_out_ref
+    base_ref, doc_ref, q_ref, k_ref, k_prev_ref, p_ref, total_ref, qt_ref
 ):
-    features = KV_HEADS * HEAD_DIM
-    v_out_ref[:BLOCK, :] = prev_ref[:, features:]
-    v_out_ref[BLOCK:, :] = v_ref[...]
     base = base_ref[0]
     query_pos = base + lax.broadcasted_iota(jnp.int32, (BLOCK, 1), 0)
     doc_first = jnp.zeros((BLOCK, 1), jnp.int32)
@@ -56,7 +53,7 @@
     key_pos = base - BLOCK + lax.broadcasted_iota(jnp.int32, (BLOCK, WIDTH), 1)
     bias = jnp.where((key_pos >= doc_first) & (key_pos <= query_pos), 0.0, NEG)
     for g in range(KV_HEADS):
-        keys = jnp.concatenate([prev_ref[:, head_cols(g)], k_ref[:, head_cols(g)]], 0)
+        keys = jnp.concatenate([k_prev_ref[:, head_cols(g)], k_ref[:, head_cols(g)]], 0)
         for h in range(GROUP):
             head = g * GROUP + h
             q = q_ref[:, head_cols(head)]
@@ -70,7 +67,7 @@
             p_ref[g, head_cols(h), :] = (e * (1.0 / total)).astype(jnp.bfloat16)
 
 
-def backward_kernel(p_ref, qt_ref, v_ref, og_far_ref, halo_ref, own_ref, og_ref, sems):
+def value_grads_kernel(p_ref, og_far_ref, dv_ref, og_ref, sems):
     copies = [
         pltpu.make_async_copy(
             og_far_ref.at[pl.ds(g * PAIRS, PAIRS)], og_ref.at[pl.ds(g * PAIRS, PAIRS)], sems.at[g]
@@ -82,18 +79,22 @@
     for copy in copies:
         copy.wait()
     for g in range(KV_HEADS):
-        vals = v_ref[:, head_cols(g)]
-        dss, ogs = [], []
+        turned = [og_ref[g * PAIRS + h // 2, :, head_cols(h % 2)].T for h in range(GROUP)]
+        dv_ref[head_cols(g), :] = dot(jnp.concatenate(turned, 1), p_ref[g])
+
+
+def key_grads_kernel(p_ref, qt_ref, v_ref, v_prev_ref, og_ref, dv_ref, halo_ref, own_ref):
+    for g in range(KV_HEADS):
+        vals = jnp.concatenate([v_prev_ref[:, head_cols(g)], v_ref[:, head_cols(g)]], 0)
+        dscores = []
         for h in range(GROUP):
             og = og_ref[g * PAIRS + h // 2, :, head_cols(h % 2)]
             dp = dot(og, vals, NT)
-            p = p_ref[g, h * BLOCK : (h + 1) * BLOCK, :].astype(jnp.float32)
+            p = p_ref[g, head_cols(h), :].astype(jnp.float32)
             delta = jnp.sum(p * dp, axis=1, keepdims=True)
-            dss.append((p * (dp - delta)).astype(jnp.bfloat16))
-            ogs.append(og.T)
-        dk = dot(qt_ref[g], jnp.concatenate(dss, 0)) * SCALE
-        dv = dot(jnp.concatenate(ogs, 1), p_ref[g])
-        for i, grad in enumerate((dk, dv)):
+            dscores.append((p * (dp - delta)).astype(jnp.bfloat16))
+        dk = dot(qt_ref[g], jnp.concatenate(dscores, 0)) * SCALE
+        for i, grad in enumerate((dk, dv_ref[head_cols(g), :])):
             halo_ref[feature_rows(g, i), :] = grad[:, :BLOCK].astype(jnp.bfloat16)
             own_ref[feature_rows(g, i), :] = grad[:, BLOCK:]
 
@@ -146,33 +147,38 @@
     og = lax.all_to_all(
         out_grad.reshape(owners, BLOCK, HEADS_OWNED * HEAD_DIM), "head", 0, 0, tiled=True
     )
-    prev = lax.ppermute(jnp.concatenate([keys, values], 1), ("span", "head"), onward)
+    k_prev = lax.ppermute(keys, ("span", "head"), onward)
+    v_prev = lax.ppermute(values, ("span", "head"), onward)
     macs = HEADS * BLOCK * BLOCK * HEAD_DIM
     array = jax.ShapeDtypeStruct
-    weights, totals, turned_queries, held_values = call(
+    weights, totals, turned_queries = call(
         forward_kernel,
         (
             array((KV_HEADS, GROUP * BLOCK, WIDTH), bf16),
             array((HEADS, BLOCK), f32),
             array((KV_HEADS, HEAD_DIM, GROUP * BLOCK), bf16),
-            array((WIDTH, KV_HEADS * HEAD_DIM), bf16),
-        ),
-        (base, doc_lengths, queries, keys, values, prev),
-        [SMEM, SMEM] + [VMEM] * 4,
+        ),
+        (base, doc_lengths, queries, keys, k_prev),
+        [SMEM, SMEM] + [VMEM] * 3,
         flops=20000 * macs,
         exps=HEADS * BLOCK * WIDTH,
     )
     features = 2 * KV_HEADS * HEAD_DIM
+    any_space = pl.BlockSpec(memory_space=pl.ANY)
+    value_grads, held_grads = call(
+        value_grads_kernel,
+        (array((KV_HEADS * HEAD_DIM, WIDTH), f32), array(og.shape, bf16)),
+        (weights, og),
+        [VMEM, any_space],
+        scratch=[pltpu.SemaphoreType.DMA((KV_HEADS,))],
+        flops=4 * macs,
+    )
     halo, own = call(
-        backward_kernel,
+        key_grads_kernel,
         (array((features, BLOCK), bf16), array((features, BLOCK), f32)),
-        (weights, turned_queries, held_values, og),
-        [VMEM] * 3 + [pl.BlockSpec(memory_space=pl.ANY)],
-        scratch=[
-            pltpu.VMEM((owners, BLOCK, HEADS_OWNED * HEAD_DIM), bf16),
-            pltpu.SemaphoreType.DMA((KV_HEADS,)),
-        ],
-        flops=12 * macs,
+        (weights, turned_queries, values, v_prev, held_grads, value_grads),
+        [VMEM] * 6,
+        flops=8 * macs,
     )
     returned = lax.ppermute(halo, ("span", "head"), back)
     send = call(

time: 117 us -> 117 us (level)
  starting transfers between devices: 24.2 us -> 28.1 us
  local copies, waits for them, and re-layouts: 4.44 us -> 1.23 us
  blocking collectives: 30.1 us -> 27.6 us
  waiting for transfers between devices: 46.5 us -> 48.5 us
  Pallas kernels: 9.18 us -> 10.4 us
    all_to_all x1, waiting for transfers between devices: 38 us -> 42.1 us  [shards(): lax.all_to_all(out_grad.reshape(owners, BLOCK, HEADS_OWNED * HEAD_DIM), '...]
    ppermute x1 -> x2, starting transfers between devices: 4.28 us -> 8.19 us  [the longest x1 4.41 us: shards(): k_prev = lax.ppermute(keys, ('span', 'head'), onward)]
    unnamed x12 -> x6, local copies, waits for them, and re-layouts: 4.44 us -> 1.23 us
    all_to_all x1, blocking collectives: 30.1 us -> 27.6 us  [shards(): got = lax.all_to_all(send, 'head', 0, 0, tiled=True)]
    ppermute x1 -> x2, waiting for transfers between devices: 2.14 us -> 0.01 us  [the longest x1 0.01 us: shards(): v_prev = lax.ppermute(values, ('span', 'head'), onward)]
    pallas_call x4 -> x5, Pallas kernels: 9.18 us -> 10.4 us  [call(): pl.pallas_call(kernel, out_shape=out_shape, in_specs=specs, out_specs=jax...]
  transfers between devices with their start and end apart: 3 -> 4, of which waited for: 3 -> 2; matrix products, arithmetic and copies ran while one was open for 0% -> 0% of each run, Pallas kernels for 4% -> 6%
where the time goes in v5:
time: 117 us
  waiting for transfers between devices  48.5 us (41%)
  starting transfers between devices  28.1 us (24%)
  blocking collectives  27.6 us (24%)
  Pallas kernels  10.4 us (9%)
  local copies, waits for them, and re-layouts  1.23 us (1%)
    all_to_all x1, waiting for transfers between devices, shards(): lax.all_to_all(out_grad.reshape(owners, BLOCK, HEADS_OWNED * HEAD_DIM), '...  42.1 us
    all_to_all x1, blocking collectives, shards(): got = lax.all_to_all(send, 'head', 0, 0, tiled=True)  27.6 us
    all_to_all x1, starting transfers between devices, shards(): lax.all_to_all(out_grad.reshape(owners, BLOCK, HEADS_OWNED * HEAD_DIM), '...  18 us
    pallas_call x5, Pallas kernels, call(): pl.pallas_call(kernel, out_shape=out_shape, in_specs=specs, out_specs=jax...  10.4 us
    ppermute x1, waiting for transfers between devices, shards(): returned = lax.ppermute(halo, ('span', 'head'), back)  6.34 us
    ppermute x1, starting transfers between devices, shards(): k_prev = lax.ppermute(keys, ('span', 'head'), onward)  4.41 us
    ppermute x1, starting transfers between devices, shards(): v_prev = lax.ppermute(values, ('span', 'head'), onward)  3.77 us
  transfers between devices with their start and end apart: 4, of which 2 were waited for; matrix products, arithmetic and copies ran while one was open for 0% of the time, Pallas kernels for 6%

profile of v5, /device:TPU:56, one launch (start us, length us, event | category | flops | bytes accessed | tf_op | source)
XLA Modules:
  0.0 116.5 jit_solution(15522313398962659756)
XLA Ops:
  0.6 0.0 copy-start.1
  0.6 0.0 copy-start.2
  0.6 4.4 %collective-permute-start = (bf16[128,512]{1,0:T(8,128)(2,1)}, bf16[128,512]{1,0:T(8,128)(2,1)S(1)}, u32[]{:S(2)}, u32[]{:S(2)}) collective-permute-start(bf16[128,512]{1,0:T(8,128)(2,1)} %k_ref.1), channel_id=1, source_target_pairs={{0,4},{4,8},{8,12},{12,16},{16,20},{20,24},{24,28},{28,32},{32,36}... | collective-permute-start | bytes 393224 | tf_op jit(solution)/shard_map/ppermute | solution.py:150
  5.1 18.0 %all-to-all-start = ((bf16[16,128,256]{2,1,0:T(8,128)(2,1)}), bf16[16,128,256]{2,1,0:T(8,128)(2,1)}, u32[]{:S(2)}, u32[]{:S(2)}) async-start(bf16[16,128,256]{2,1,0:T(8,128)(2,1)} %bitcast.2), calls=%async_computation | async-start | bytes 2097152 | tf_op jit(solution)/shard_map/all_to_all | solution.py:147
  23.1 3.8 %collective-permute-start.1 = (bf16[128,512]{1,0:T(8,128)(2,1)}, bf16[128,512]{1,0:T(8,128)(2,1)}, u32[]{:S(2)}, u32[]{:S(2)}) collective-permute-start(bf16[128,512]{1,0:T(8,128)(2,1)} %v_ref.1), channel_id=1, source_target_pairs={{0,4},{4,8},{8,12},{12,16},{16,20},{20,24},{24,28},{28,32},{32,36}... | collective-permute-start | bytes 393224 | tf_op jit(solution)/shard_map/ppermute | solution.py:151
  26.9 0.0 collective-permute-done.k_prev_ref
  26.9 0.0 copy-done.1
  26.9 0.0 copy-done.2
  26.9 0.0 copy-start
  26.9 1.2 %copy-done = bf16[128,4096]{1,0:T(8,128)(2,1)S(1)} copy-done((bf16[128,4096]{1,0:T(8,128)(2,1)S(1)}, bf16[128,4096]{1,0:T(8,128)(2,1)}, u32[]{:S(2)}) %copy-start) | copy-done | bytes 1048600
  28.2 5.1 %shard_map.68 = (bf16[4,1024,256]{2,1,0:T(8,128)(2,1)S(1)}, f32[32,128]{1,0:T(8,128)S(1)}, bf16[4,128,1024]{2,1,0:T(8,128)(2,1)S(1)}) custom-call(s32[1]{0:T(128)} %bitcast.base_ref, s32[32]{0:T(128)S(1)} %copy-done.2, bf16[128,4096]{1,0:T(8,128)(2,1)S(1)} %copy-done, bf16[128,512]{1,0:T(8,128)(2,1)S(1)} %copy-done.1, ...), custom_call_target="tpu_custom_call" | custom-call | flops 1342177280000 | bytes 4472964 | tf_op jit(solution)/shard_map/pallas_call | solution.py:126
  33.3 42.1 %all-to-all-done.og_far_ref = bf16[16,128,256]{2,1,0:T(8,128)(2,1)} async-done(((bf16[16,128,256]{2,1,0:T(8,128)(2,1)}), bf16[16,128,256]{2,1,0:T(8,128)(2,1)}, u32[]{:S(2)}, u32[]{:S(2)}) %all-to-all-start) | async-done | bytes 1048608 | tf_op jit(solution)/shard_map/all_to_all | solution.py:147
  75.4 1.7 %shard_map.69 = (f32[512,256]{1,0:T(8,128)S(1)}, bf16[16,128,256]{2,1,0:T(8,128)(2,1)S(1)}) custom-call(bf16[4,1024,256]{2,1,0:T(8,128)(2,1)S(1)} %get-tuple-element.9.p_ref, bf16[16,128,256]{2,1,0:T(8,128)(2,1)} %all-to-all-done.og_far_ref), custom_call_target="tpu_custom_call" | custom-call | flops 268435456 | bytes 4718592 | tf_op jit(solution)/shard_map/pallas_call | solution.py:126
  77.1 0.0 collective-permute-done.1.v_prev_ref
  77.1 2.7 %shard_map.70 = (bf16[1024,128]{1,0:T(8,128)(2,1)S(1)}, f32[1024,128]{1,0:T(8,128)S(1)}) custom-call(bf16[4,1024,256]{2,1,0:T(8,128)(2,1)S(1)} %get-tuple-element.9.p_ref, bf16[4,128,1024]{2,1,0:T(8,128)(2,1)S(1)} %get-tuple-element.10.qt_ref, bf16[128,512]{1,0:T(8,128)(2,1)} %v_ref.1, bf16[128,512]{1,0:T(8,128)(2,1)} %collective-permute-done.1.v_prev_ref, ...), custom_call_target="tpu_custom_call" | custom-call | flops 536870912 | bytes 5767168 | tf_op jit(solution)/shard_map/pallas_call | solution.py:126
  79.9 1.9 %collective-permute-start.2 = (bf16[1024,128]{1,0:T(8,128)(2,1)S(1)}, bf16[1024,128]{1,0:T(8,128)(2,1)S(1)}, u32[]{:S(2)}, u32[]{:S(2)}) collective-permute-start(bf16[1024,128]{1,0:T(8,128)(2,1)S(1)} %get-tuple-element.14), channel_id=1, source_target_pairs={{4,0},{8,4},{12,8},{16,12},{20,16},{24,20},{28,24},{32,28},{36,32}... | collective-permute-start | bytes 786440 | tf_op jit(solution)/shard_map/ppermute | solution.py:183
  81.8 6.3 %collective-permute-done.2.halo_ref = bf16[1024,128]{1,0:T(8,128)(2,1)S(1)} collective-permute-done((bf16[1024,128]{1,0:T(8,128)(2,1)S(1)}, bf16[1024,128]{1,0:T(8,128)(2,1)S(1)}, u32[]{:S(2)}, u32[]{:S(2)}) %collective-permute-start.2) | collective-permute-done | bytes 262176 | tf_op jit(solution)/shard_map/ppermute | solution.py:183
  88.1 0.1 shard_map.71
  88.2 27.6 %all_to_all.10.got_ref = bf16[16,72,128]{2,1,0:T(8,128)(2,1)S(1)} all-to-all(bf16[16,72,128]{2,1,0:T(8,128)(2,1)S(1)} %shard_map.71), channel_id=1, replica_groups=mesh['span'=16,'head'=16,'rep'=4] {'head'}, dimensions={0} | all-to-all | bytes 589824 | tf_op jit(solution)/shard_map/all_to_all | solution.py:190
  115.8 0.8 shard_map.72
Async XLA Ops:
  0.6 26.3 %copy-start.1 = (bf16[128,512]{1,0:T(8,128)(2,1)S(1)}, bf16[128,512]{1,0:T(8,128)(2,1)}, u32[]{:S(2)}) copy-start(bf16[128,512]{1,0:T(8,128)(2,1)} %k_ref.1) | copy-start | bytes 393220
  0.6 26.3 %copy-start.2 = (s32[32]{0:T(128)S(1)}, s32[32]{0:T(128)}, u32[]{:S(2)}) copy-start(s32[32]{0:T(128)} %doc_ref.1) | copy-start | bytes 388
  0.6 26.2 %collective-permute-start = (bf16[128,512]{1,0:T(8,128)(2,1)}, bf16[128,512]{1,0:T(8,128)(2,1)S(1)}, u32[]{:S(2)}, u32[]{:S(2)}) collective-permute-start(bf16[128,512]{1,0:T(8,128)(2,1)} %k_ref.1), channel_id=1, source_target_pairs={{0,4},{4,8},{8,12},{12,16},{16,20},{20,24},{24,28},{28,32},{32,36}... | collective-permute-start | bytes 393224 | tf_op jit(solution)/shard_map/ppermute | solution.py:150
  5.1 70.3 %all-to-all-start = ((bf16[16,128,256]{2,1,0:T(8,128)(2,1)}), bf16[16,128,256]{2,1,0:T(8,128)(2,1)}, u32[]{:S(2)}, u32[]{:S(2)}) async-start(bf16[16,128,256]{2,1,0:T(8,128)(2,1)} %bitcast.2), calls=%async_computation | async-start | bytes 2097152 | tf_op jit(solution)/shard_map/all_to_all | solution.py:147
  23.1 54.0 %collective-permute-start.1 = (bf16[128,512]{1,0:T(8,128)(2,1)}, bf16[128,512]{1,0:T(8,128)(2,1)}, u32[]{:S(2)}, u32[]{:S(2)}) collective-permute-start(bf16[128,512]{1,0:T(8,128)(2,1)} %v_ref.1), channel_id=1, source_target_pairs={{0,4},{4,8},{8,12},{12,16},{16,20},{20,24},{24,28},{28,32},{32,36}... | collective-permute-start | bytes 393224 | tf_op jit(solution)/shard_map/ppermute | solution.py:151
  26.9 1.2 %copy-start = (bf16[128,4096]{1,0:T(8,128)(2,1)S(1)}, bf16[128,4096]{1,0:T(8,128)(2,1)}, u32[]{:S(2)}) copy-start(bf16[128,4096]{1,0:T(8,128)(2,1)} %q_ref.1) | copy-start | bytes 3145732
  79.9 8.3 %collective-permute-start.2 = (bf16[1024,128]{1,0:T(8,128)(2,1)S(1)}, bf16[1024,128]{1,0:T(8,128)(2,1)S(1)}, u32[]{:S(2)}, u32[]{:S(2)}) collective-permute-start(bf16[1024,128]{1,0:T(8,128)(2,1)S(1)} %get-tuple-element.14), channel_id=1, source_target_pairs={{4,0},{8,4},{12,8},{16,12},{20,16},{24,20},{28,24},{32,28},{36,32}... | collective-permute-start | bytes 786440 | tf_op jit(solution)/shard_map/ppermute | solution.py:183

commit v6 on v4

--- a/solution.py
+++ b/solution.py
@@ -43,8 +43,7 @@
 def forward_kernel(
     base_ref, doc_ref, q_ref, k_ref, v_ref, prev_ref, p_ref, total_ref, qt_ref, v_out_ref
 ):
-    features = KV_HEADS * HEAD_DIM
-    v_out_ref[:BLOCK, :] = prev_ref[:, features:]
+    v_out_ref[:BLOCK, :] = prev_ref[BLOCK:, :]
     v_out_ref[BLOCK:, :] = v_ref[...]
     base = base_ref[0]
     query_pos = base + lax.broadcasted_iota(jnp.int32, (BLOCK, 1), 0)
@@ -56,7 +55,7 @@
     key_pos = base - BLOCK + lax.broadcasted_iota(jnp.int32, (BLOCK, WIDTH), 1)
     bias = jnp.where((key_pos >= doc_first) & (key_pos <= query_pos), 0.0, NEG)
     for g in range(KV_HEADS):
-        keys = jnp.concatenate([prev_ref[:, head_cols(g)], k_ref[:, head_cols(g)]], 0)
+        keys = jnp.concatenate([prev_ref[:BLOCK, head_cols(g)], k_ref[:, head_cols(g)]], 0)
         for h in range(GROUP):
             head = g * GROUP + h
             q = q_ref[:, head_cols(head)]
@@ -111,22 +110,32 @@
         send_ref[z, OWNED:, :] = jnp.concatenate([high, low, pad], 0).astype(jnp.bfloat16)
 
 
-def unpack_kernel(got_ref, grads_ref, total_ref):
+def unpack_kernel(got_ref, grads_ref, total_ref, sems):
+    copies = [
+        pltpu.make_async_copy(
+            got_ref.at[b, pl.ds(0, OWNED)], grads_ref.at[:, pl.ds(b * BLOCK, BLOCK)], sems.at[b]
+        )
+        for b in range(OWNERS)
+    ]
+    for copy in copies:
+        copy.start()
     for b in range(OWNERS):
-        cols = slice(b * BLOCK, (b + 1) * BLOCK)
-        grads_ref[:, cols] = got_ref[b, :OWNED, :]
         extra = got_ref[b, OWNED:, :].astype(jnp.float32)
-        total_ref[:, cols] = extra[:HEADS_OWNED] + extra[HEADS_OWNED : 2 * HEADS_OWNED]
-
-
-def call(kernel, out_shape, args, specs, scratch=(), flops=0, exps=0, limit=8):
+        total_ref[:, b * BLOCK : (b + 1) * BLOCK] = (
+            extra[:HEADS_OWNED] + extra[HEADS_OWNED : 2 * HEADS_OWNED]
+        )
+    for copy in copies:
+        copy.wait()
+
+
+def call(kernel, out_shape, args, specs, scratch=(), out_specs=None, flops=0, exps=0, limit=8):
     outs = jax.tree.leaves(out_shape)
     moved = sum(math.prod(a.shape) * a.dtype.itemsize for a in [*args, *outs])
     return pl.pallas_call(
         kernel,
         out_shape=out_shape,
         in_specs=specs,
-        out_specs=jax.tree.map(lambda _: VMEM, out_shape),
+        out_specs=out_specs or jax.tree.map(lambda _: VMEM, out_shape),
         scratch_shapes=scratch,
         compiler_params=pltpu.CompilerParams(vmem_limit_bytes=limit * 2**20),
         cost_estimate=pl.CostEstimate(
@@ -146,7 +155,7 @@
     og = lax.all_to_all(
         out_grad.reshape(owners, BLOCK, HEADS_OWNED * HEAD_DIM), "head", 0, 0, tiled=True
     )
-    prev = lax.ppermute(jnp.concatenate([keys, values], 1), ("span", "head"), onward)
+    prev = lax.ppermute(jnp.concatenate([keys, values], 0), ("span", "head"), onward)
     macs = HEADS * BLOCK * BLOCK * HEAD_DIM
     array = jax.ShapeDtypeStruct
     weights, totals, turned_queries, held_values = call(
@@ -190,6 +199,8 @@
         ),
         (got,),
         [VMEM],
+        scratch=[pltpu.SemaphoreType.DMA((OWNERS,))],
+        out_specs=(pl.BlockSpec(memory_space=pl.ANY), VMEM),
     )
 
 

time: 117 us -> 117 us (level)
  no operation moved by 1% of the time
where the time goes in v6:
time: 117 us
  waiting for transfers between devices  46.5 us (40%)
  blocking collectives  30.1 us (26%)
  starting transfers between devices  24.2 us (21%)
  Pallas kernels  9.87 us (8%)
  local copies, waits for them, and re-layouts  4.44 us (4%)
    all_to_all x1, waiting for transfers between devices, shards(): lax.all_to_all(out_grad.reshape(owners, BLOCK, HEADS_OWNED * HEAD_DIM), '...  38 us
    all_to_all x1, blocking collectives, shards(): got = lax.all_to_all(send, 'head', 0, 0, tiled=True)  30.1 us
    all_to_all x1, starting transfers between devices, shards(): lax.all_to_all(out_grad.reshape(owners, BLOCK, HEADS_OWNED * HEAD_DIM), '...  18 us
    pallas_call x4, Pallas kernels, call(): pl.pallas_call(kernel, out_shape=out_shape, in_specs=specs, out_specs=out...  9.87 us
    ppermute x1, waiting for transfers between devices, shards(): returned = lax.ppermute(halo, ('span', 'head'), back)  6.34 us
    unnamed x12, local copies, waits for them, and re-layouts  4.44 us
    ppermute x1, starting transfers between devices, shards(): lax.ppermute(jnp.concatenate([keys, values], 0), ('span', 'head'), onward)  4.28 us
  transfers between devices with their start and end apart: 3, of which 3 were waited for; matrix products, arithmetic and copies ran while one was open for 0% of the time, Pallas kernels for 4%

profile of v6, /device:TPU:56, one launch (start us, length us, event | category | flops | bytes accessed | tf_op | source)
XLA Modules:
  0.0 116.9 jit_solution(16494369608948967145)
XLA Ops:
  0.6 0.0 copy-start
  0.6 1.0 pad_maximum_fusion
  1.7 4.3 %collective-permute-start = (bf16[256,512]{1,0:T(8,128)(2,1)S(1)}, bf16[256,512]{1,0:T(8,128)(2,1)S(1)}, u32[]{:S(2)}, u32[]{:S(2)}) collective-permute-start(bf16[256,512]{1,0:T(8,128)(2,1)S(1)} %pad_maximum_fusion), channel_id=1, source_target_pairs={{0,4},{4,8},{8,12},{12,16},{16,20},{20,24},{24,28},{28,32},{32,36}... | collective-permute-start | bytes 786440 | tf_op jit(solution)/shard_map/ppermute | solution.py:158
  6.0 18.0 %all-to-all-start = ((bf16[16,128,256]{2,1,0:T(8,128)(2,1)}), bf16[16,128,256]{2,1,0:T(8,128)(2,1)}, u32[]{:S(2)}, u32[]{:S(2)}) async-start(bf16[16,128,256]{2,1,0:T(8,128)(2,1)} %bitcast.2), calls=%async_computation | async-start | bytes 2097152 | tf_op jit(solution)/shard_map/all_to_all | solution.py:155
  24.0 2.1 %collective-permute-done.prev_ref = bf16[256,512]{1,0:T(8,128)(2,1)S(1)} collective-permute-done((bf16[256,512]{1,0:T(8,128)(2,1)S(1)}, bf16[256,512]{1,0:T(8,128)(2,1)S(1)}, u32[]{:S(2)}, u32[]{:S(2)}) %collective-permute-start) | collective-permute-done | bytes 262176 | tf_op jit(solution)/shard_map/ppermute | solution.py:158
  26.1 0.0 copy-start.3
  26.1 0.7 copy-done.3
  26.8 0.0 copy-done
  26.8 0.0 copy-start.1
  26.8 0.9 copy-done.1
  27.7 0.0 copy-start.2
  27.8 1.2 %copy-done.2 = bf16[128,4096]{1,0:T(8,128)(2,1)S(1)} copy-done((bf16[128,4096]{1,0:T(8,128)(2,1)S(1)}, bf16[128,4096]{1,0:T(8,128)(2,1)}, u32[]{:S(2)}) %copy-start.2) | copy-done | bytes 1048600
  29.0 0.0 copy-start.4
  29.0 0.9 copy-done.4
  29.9 0.0 copy-start.5
  29.9 0.7 copy-done.5
  30.6 5.1 %shard_map.68 = (bf16[4,1024,256]{2,1,0:T(8,128)(2,1)S(1)}, f32[32,128]{1,0:T(8,128)S(1)}, bf16[4,128,1024]{2,1,0:T(8,128)(2,1)S(1)}, bf16[256,512]{1,0:T(8,128)(2,1)S(1)}) custom-call(s32[1]{0:T(128)} %bitcast.base_ref, s32[32]{0:T(128)S(1)} %copy-done.5, bf16[128,4096]{1,0:T(8,128)(2,1)S(1)} %copy-done.2, bf16[128,512]{1,0:T(8,128)(2,1)S(1)} %copy-done, ...), custom_call_target="tpu_custom_call" | custom-call | flops 1342177280000 | bytes 4997252 | tf_op jit(solution)/shard_map/pallas_call | solution.py:134
  35.7 38.0 %all-to-all-done.og_far_ref = bf16[16,128,256]{2,1,0:T(8,128)(2,1)} async-done(((bf16[16,128,256]{2,1,0:T(8,128)(2,1)}), bf16[16,128,256]{2,1,0:T(8,128)(2,1)}, u32[]{:S(2)}, u32[]{:S(2)}) %all-to-all-start) | async-done | bytes 1048608 | tf_op jit(solution)/shard_map/all_to_all | solution.py:155
  73.7 3.2 %shard_map.69 = (bf16[1024,128]{1,0:T(8,128)(2,1)S(1)}, f32[1024,128]{1,0:T(8,128)S(1)}) custom-call(bf16[4,1024,256]{2,1,0:T(8,128)(2,1)S(1)} %get-tuple-element.8.p_ref, bf16[4,128,1024]{2,1,0:T(8,128)(2,1)S(1)} %get-tuple-element.9.qt_ref, bf16[256,512]{1,0:T(8,128)(2,1)S(1)} %get-tuple-element.10.v_ref, bf16[16,128,256]{2,1,0:T(8,128)(2,1)} %all-to-all-done.og_far_ref), custom_call_target="tpu_custom_call" | custom-call | flops 805306368 | bytes 5242880 | tf_op jit(solution)/shard_map/pallas_call | solution.py:134
  77.0 1.9 %collective-permute-start.1 = (bf16[1024,128]{1,0:T(8,128)(2,1)S(1)}, bf16[1024,128]{1,0:T(8,128)(2,1)S(1)}, u32[]{:S(2)}, u32[]{:S(2)}) collective-permute-start(bf16[1024,128]{1,0:T(8,128)(2,1)S(1)} %get-tuple-element.12), channel_id=1, source_target_pairs={{4,0},{8,4},{12,8},{16,12},{20,16},{24,20},{28,24},{32,28},{36,32}... | collective-permute-start | bytes 786440 | tf_op jit(solution)/shard_map/ppermute | solution.py:186
  78.9 6.3 %collective-permute-done.1.halo_ref = bf16[1024,128]{1,0:T(8,128)(2,1)S(1)} collective-permute-done((bf16[1024,128]{1,0:T(8,128)(2,1)S(1)}, bf16[1024,128]{1,0:T(8,128)(2,1)S(1)}, u32[]{:S(2)}, u32[]{:S(2)}) %collective-permute-start.1) | collective-permute-done | bytes 262176 | tf_op jit(solution)/shard_map/ppermute | solution.py:186
  85.2 0.1 shard_map.70
  85.3 30.1 %all_to_all.10.got_ref = bf16[16,72,128]{2,1,0:T(8,128)(2,1)S(1)} all-to-all(bf16[16,72,128]{2,1,0:T(8,128)(2,1)S(1)} %shard_map.70), channel_id=1, replica_groups=mesh['span'=16,'head'=16,'rep'=4] {'head'}, dimensions={0} | all-to-all | bytes 589824 | tf_op jit(solution)/shard_map/all_to_all | solution.py:193
  115.4 1.4 %shard_map.71 = (bf16[64,2048]{1,0:T(8,128)(2,1)}, f32[2,2048]{1,0:T(2,128)}) custom-call(bf16[16,72,128]{2,1,0:T(8,128)(2,1)S(1)} %all_to_all.10.got_ref), custom_call_target="tpu_custom_call" | custom-call | bytes 573440 | tf_op jit(solution)/shard_map/pallas_call | solution.py:134
Async XLA Ops:
  0.6 26.2 %copy-start = (bf16[128,512]{1,0:T(8,128)(2,1)S(1)}, bf16[128,512]{1,0:T(8,128)(2,1)}, u32[]{:S(2)}) copy-start(bf16[128,512]{1,0:T(8,128)(2,1)} %k_ref.1) | copy-start | bytes 393220
  1.7 24.5 %collective-permute-start = (bf16[256,512]{1,0:T(8,128)(2,1)S(1)}, bf16[256,512]{1,0:T(8,128)(2,1)S(1)}, u32[]{:S(2)}, u32[]{:S(2)}) collective-permute-start(bf16[256,512]{1,0:T(8,128)(2,1)S(1)} %pad_maximum_fusion), channel_id=1, source_target_pairs={{0,4},{4,8},{8,12},{12,16},{16,20},{20,24},{24,28},{28,32},{32,36}... | collective-permute-start | bytes 786440 | tf_op jit(solution)/shard_map/ppermute | solution.py:158
  6.0 67.7 %all-to-all-start = ((bf16[16,128,256]{2,1,0:T(8,128)(2,1)}), bf16[16,128,256]{2,1,0:T(8,128)(2,1)}, u32[]{:S(2)}, u32[]{:S(2)}) async-start(bf16[16,128,256]{2,1,0:T(8,128)(2,1)} %bitcast.2), calls=%async_computation | async-start | bytes 2097152 | tf_op jit(solution)/shard_map/all_to_all | solution.py:155
  26.1 0.7 copy-start.3
  26.8 0.9 copy-start.1
  27.7 1.2 %copy-start.2 = (bf16[128,4096]{1,0:T(8,128)(2,1)S(1)}, bf16[128,4096]{1,0:T(8,128)(2,1)}, u32[]{:S(2)}) copy-start(bf16[128,4096]{1,0:T(8,128)(2,1)} %q_ref.1) | copy-start | bytes 3145732
  29.0 0.9 copy-start.4
  29.9 0.7 copy-start.5
  77.0 8.3 %collective-permute-start.1 = (bf16[1024,128]{1,0:T(8,128)(2,1)S(1)}, bf16[1024,128]{1,0:T(8,128)(2,1)S(1)}, u32[]{:S(2)}, u32[]{:S(2)}) collective-permute-start(bf16[1024,128]{1,0:T(8,128)(2,1)S(1)} %get-tuple-element.12), channel_id=1, source_target_pairs={{4,0},{8,4},{12,8},{16,12},{20,16},{24,20},{28,24},{32,28},{36,32}... | collective-permute-start | bytes 786440 | tf_op jit(solution)/shard_map/ppermute | solution.py:186
